TPU v7x, 128 devices: a whole 4x4x4 slice. The times are simulated.
128 devices in a mesh: space: 16 (over y, x), sub: 8 (over z, core).
Axes of the slice: x: 4, y: 4, z: 4, core: 2. Of those that a mesh axis runs over, the one named last changes fastest.
Arguments:
- seg_data: float32 [4096, 9, 128], P(('space', 'sub')), as said below
- cell_of_block: int32 [4096], P(('space', 'sub')), may hold values from 0 to 4095, as said below
- cell_center: float32 [3, 4096], replicated, as said below
- pairs: int32 [16384, 2], P(('space', 'sub')), may hold values from 0 to 4095, as said below
- live_count: int32 [128], P(('space', 'sub')), may hold values from 1 to 128, as said below
Outputs:
- force: float32 [4096, 3, 128], P(('space', 'sub'))
Inputs may be any that keep to these rules, and one draw needn't show every extreme that they name: `seg_data`: offsets, line and Burgers vector components of the segments. cell_of_block[g] lies in the range of cells of the region of g's owner: its space index times 4096 / 16 and up. `cell_center`: coordinates of the cell centres. `pairs`: every slot of device d (live or not) has as target a block of d and as source a different block whose owner's space index differs from d's by at most one, cyclically. `live_count`: some device has all 128 slots live.
All inputs are finite; a program needn't handle non-finite values.
Results may differ from a plain program's by a relative error of at most 0.0003.
Values sent between devices are 32-bit elements; how exact they have to be, the bound alone decides.
A program may use at most 64 MiB of HBM per device.

v0:
```python
import jax
import jax.numpy as jnp
from jax import lax
from jax.sharding import PartitionSpec as P

NBATCH = 32


near_a2 = 0.25
far_a2 = 1.0
group_blocks = 4
highest = lax.Precision.HIGHEST


def with_halo(shard, sides, width):
    for axis, dim in sides:
        devices, length = (lax.axis_size(axis), shard.shape[dim])
        up = [(i, (i + 1) % devices) for i in range(devices)]
        down = [(j, i) for i, j in up]
        last = lax.slice_in_dim(shard, length - width, length, axis=dim)
        initial = lax.slice_in_dim(shard, 0, width, axis=dim)
        before = lax.ppermute(last, axis, up)
        after = lax.ppermute(initial, axis, down)
        shard = jnp.concatenate([before, shard, after], axis=dim)
    return shard


def from_behind(shard, axis, by):
    devices = lax.axis_size(axis)
    return lax.ppermute(shard, axis, [(i, (i + by) % devices) for i in range(devices)])


def pair_forces(left, right):
    apart = left[:, 0:3, :, None] - right[:, 0:3, None, :]
    dist2 = jnp.sum(apart * apart, axis=1) + near_a2
    weight = 1.0 / (dist2 * jnp.sqrt(dist2))
    cross_one = jnp.einsum("nki,nkj->nij", left[:, 6:9], right[:, 3:6], precision=highest)
    cross_two = jnp.einsum("nki,nkj->nij", left[:, 3:6], right[:, 6:9], precision=highest)
    coupling = weight * cross_one * cross_two
    pushed = coupling[:, None] * apart
    return (jnp.sum(pushed, axis=3), -jnp.sum(pushed, axis=2))


def far_group(block_data, block_cells, moments, cell_center):
    count = block_data.shape[0]
    width = block_data.shape[2]
    ncell = cell_center.shape[1]
    flat = block_data.transpose(1, 0, 2).reshape(9, count * width)
    seg_cell = jnp.repeat(block_cells, width)
    dist2 = jnp.zeros((ncell, count * width), jnp.float32)
    for axis_k in range(3):
        delta = cell_center[axis_k][:, None] - flat[axis_k][None, :]
        dist2 = dist2 + delta * delta
    weight = 1.0 / (far_a2 + dist2)
    same = jnp.arange(ncell, dtype=jnp.int32)[:, None] == seg_cell[None, :]
    weight = jnp.where(same, 0.0, weight)
    grid = jnp.dot(moments, weight, precision=highest)
    result = jnp.sum(grid.reshape(3, 3, -1) * flat[None, 3:6, :], axis=1)
    return result.reshape(3, count, width).transpose(1, 0, 2)


def on_device(seg_data, cell_of_block, cell_center, pairs, live_count):
    nblocks = seg_data.shape[0]
    width = seg_data.shape[2]
    ncell = cell_center.shape[1]
    nspace = lax.axis_size("space")
    nsub = lax.axis_size("sub")
    my_space = lax.axis_index("space")
    onehot = (cell_of_block[:, None] == jnp.arange(ncell, dtype=jnp.int32)[None, :]).astype(
        jnp.float32
    )
    centre = jnp.dot(onehot, cell_center.T, precision=highest)
    packed = jnp.concatenate(
        [seg_data[:, 0:3, :] + centre[:, :, None], seg_data[:, 3:9, :]], axis=1
    )
    column = nsub * nblocks
    gathered = lax.all_gather(packed, "sub", axis=0, tiled=True)
    window = with_halo(gathered, (("space", 0),), column)
    count = live_count[0]

    def window_index(block):
        region = block // nblocks // nsub
        place = (region - my_space + 1) % nspace
        return place * column + (block - region * column)

    targets = window_index(pairs[:, 0])
    sources = window_index(pairs[:, 1])
    turns = (count + NBATCH - 1) // NBATCH

    def add_batch(step, total):
        start = step * NBATCH
        tgt = lax.dynamic_slice_in_dim(targets, start, NBATCH)
        src = lax.dynamic_slice_in_dim(sources, start, NBATCH)
        alive = (start + jnp.arange(NBATCH, dtype=jnp.int32) < count).astype(jnp.float32)
        on_left, on_right = pair_forces(window[tgt], window[src])
        total = total.at[tgt].add(on_left * alive[:, None, None])
        return total.at[src].add(on_right * alive[:, None, None])

    acc = lax.fori_loop(0, turns, add_batch, jnp.zeros((3 * column, 3, width), jnp.float32))
    thirds = acc.reshape(3, column, 3, width)
    from_above = from_behind(thirds[0], "space", -1)
    from_below = from_behind(thirds[2], "space", 1)
    near = lax.psum_scatter(
        thirds[1] + from_above + from_below, "sub", scatter_dimension=0, tiled=True
    )
    outer = jnp.einsum("gas,gbs->gab", packed[:, 6:9], packed[:, 3:6], precision=highest)
    local_moments = jnp.dot(outer.reshape(nblocks, 9).T, onehot, precision=highest)
    moments = lax.psum(local_moments, ("space", "sub"))

    def one_group(item):
        return far_group(item[0], item[1], moments, cell_center)

    far = lax.map(
        one_group,
        (
            packed.reshape(nblocks // group_blocks, group_blocks, 9, width),
            cell_of_block.reshape(nblocks // group_blocks, group_blocks),
        ),
    )
    return near + far.reshape(nblocks, 3, width)


def solution(mesh):
    placed = (
        P(("space", "sub"), None, None),
        P(("space", "sub")),
        P(),
        P(("space", "sub"), None),
        P(("space", "sub")),
    )
    return jax.shard_map(
        on_device,
        mesh=mesh,
        in_specs=placed,
        out_specs=P(("space", "sub"), None, None),
        check_vma=False,
    )
```

profile of v0, /device:TPU:32, one launch (start us, length us, event | category | flops | bytes accessed | tf_op | source)
XLA Modules:
  0.0 406.3 jit_solution(11719518673181045841)
XLA Ops:
  7.4 0.9 slice.77
  8.3 1.3 fusion.39
  9.5 0.9 fusion.54
  10.5 0.7 pad_maximum_fusion.1
  11.2 24.2 %all-gather.2.cloned.1.call-done = f32[256,9,128]{2,0,1:T(8,128)} async-done(((f32[32,9,128]{2,0,1:T(8,128)}), f32[256,9,128]{2,0,1:T(8,128)}) %all-gather.2.cloned.1.call-update) | async-done | bytes 1179664 | tf_op jit(solution)/shard_map/all_gather | solution.py:77
  35.4 4.9 %collective-permute-start.1 = (f32[256,9,128]{2,0,1:T(8,128)}, f32[256,9,128]{2,0,1:T(8,128)S(1)}, u32[]{:S(2)}, u32[]{:S(2)}) collective-permute-start(f32[256,9,128]{2,0,1:T(8,128)} %all-gather.2.cloned.1.call-done), channel_id=1, source_target_pairs={{8,0},{16,8},{24,16},{32,24},{40,32},{48,40},{56,48},{64,56},{72,6... | collective-permute-start | bytes 3538952 | tf_op jit(solution)/shard_map/ppermute | solution.py:23
  40.9 0.8 fusion.49
  41.7 24.5 %collective-permute-done.1 = f32[256,9,128]{2,0,1:T(8,128)S(1)} collective-permute-done((f32[256,9,128]{2,0,1:T(8,128)}, f32[256,9,128]{2,0,1:T(8,128)S(1)}, u32[]{:S(2)}, u32[]{:S(2)}) %collective-permute-start.1) | collective-permute-done | bytes 1179680 | tf_op jit(solution)/shard_map/ppermute | solution.py:23
  66.2 5.4 %collective-permute-done = f32[256,9,128]{2,0,1:T(8,128)S(1)} collective-permute-done((f32[256,9,128]{2,0,1:T(8,128)}, f32[256,9,128]{2,0,1:T(8,128)S(1)}, u32[]{:S(2)}, u32[]{:S(2)}) %collective-permute-start) | collective-permute-done | bytes 1179680 | tf_op jit(solution)/shard_map/ppermute | solution.py:22
  71.6 1.5 pad_maximum_fusion
  73.1 4.9 %copy.24 = f32[768,9,128]{2,1,0:T(8,128)} copy(f32[768,9,128]{2,0,1:T(8,128)S(1)} %pad_maximum_fusion) | data formatting | bytes 7077888 | tf_op jit(solution)/shard_map/while | solution.py:99
  78.2 24.8 %while.20 = (s32[]{:T(128)}, f32[768,3,128]{2,1,0:T(4,128)S(1)}, s32[]{:T(128)}, s32[128]{0:T(128)S(1)}, f32[768,9,128]{2,1,0:T(8,128)}, /*index=5*/s32[128]{0:T...) while((s32[]{:T(128)}, f32[768,3,128]{2,1,0:T(4,128)S(1)}, s32[]{:T(128)}, ...), condition=%wide.region_6.7_spmd, body=%wide.region_0.6_spmd.sunk | while | flops 50895140 | bytes 14427815 | solution.py:99
  78.4 0.7 compare_convert_fusion.2
  79.2 3.4 gather_fusion
  82.6 3.4 gather_fusion.1
  85.9 2.1 fusion.76
  88.0 3.4 fusion.75
  91.5 4.0 fusion.77
  95.5 4.1 %fusion.78 = (f32[32,3,128]{2,1,0:T(4,128)S(1)}, f32[32,3,128]{2,1,0:T(4,128)S(1)}) fusion(f32[32,128,128]{2,1,0:T(8,128)S(1)} %fusion.77, f32[32,3,128]{2,1,0:T(4,128)S(1)} %slice.145, f32[32,3,128]{2,1,0:T(4,128)S(1)} %slice.146), kind=kLoop, calls=%fused_computation.42.clone.1 | loop fusion | flops 6266880 | bytes 2293760 | tf_op jit(solution)/shard_map/while/body/reduce_sum | solution.py:41
  99.7 1.6 scatter_fusion
  101.3 1.6 scatter_fusion.1
  103.2 0.4 collective-permute-start.2
  103.5 70.5 %collective-permute-start.3 = (f32[256,3,128]{2,0,1:T(8,128)S(1)}, f32[256,3,128]{2,0,1:T(8,128)S(1)}, u32[]{:S(2)}, u32[]{:S(2)}) collective-permute-start(f32[256,3,128]{2,0,1:T(8,128)S(1)} %get-tuple-element.142), channel_id=1, source_target_pairs={{0,8},{8,16},{16,24},{24,32},{32,40},{40,48},{48,56},{56,64},{64,7... | collective-permute-start | bytes 1179656 | tf_op jit(solution)/shard_map/ppermute | solution.py:30
  174.1 0.4 fusion.43
  174.5 1.1 fusion.38
  175.6 0.3 reduce-scatter.2.cloned.1.call-start
  176.0 3.7 collective-permute-done.2
  179.7 2.1 collective-permute-done.3
  181.8 0.8 fusion.40
  182.6 137.7 %all-reduce.2.cloned.1.call-done = f32[9,4096]{1,0:T(8,128)} async-done(((f32[9,4096]{1,0:T(8,128)}), f32[9,4096]{1,0:T(8,128)}) %all-reduce.2.cloned.1.call-update) | async-done | bytes 147472 | tf_op jit(solution)/shard_map/psum | solution.py:108
  320.3 77.1 %while.21 = (s32[]{:T(128)}, f32[8,4,3,128]{3,1,0,2:T(4,128)S(1)}, s32[8,4]{1,0:T(8,128)S(1)}, f32[3,4096]{1,0:T(4,128)S(1)}, f32[8,4,9,128]{3,1,0,2:T(4,128)}, /*index=5*/f32[9,4096]{1,0:T(8,128)}, s32[]{:T(128)}) while((s32[]{:T(128)}, f32[8,4,3,128]{3,1,0,2:T(4,128)S(1)}, s32[8,4]{1,0:T(8,128)S(1)}, f32[3,4096]{1,0:T(4,128)S(1)}, ...), condition=%wide.region_11.12_spmd, body=%wide.region_9.11_spmd.sunk | while | flops 251665920 | bytes 479377 | solution.py:113
  320.4 0.7 dynamic-slice_bitcast_fusion.2
  321.2 8.7 %fusion.83 = f32[9,512]{1,0:T(8,128)S(1)} fusion(f32[9,4096]{1,0:T(8,128)} %get-tuple-element.305, f32[512]{0:T(512)S(1)} %get-tuple-element.247, f32[4096]{0:T(1024)S(1)} %bitcast.94, f32[512]{0:T(512)S(1)} %get-tuple-element.249, f32[4096]{0:T(1024)S(1)} %bitcast.95, f32[512]{0:T(512)S(1)} %get-tuple-element.251, f32[4096]{0:T(1024)S(1)} %bitcast.93, ...), kind=kOutput, calls=%fused_computation.26.clone.1 | convolution fusion | flops 251658240 | bytes 223232 | tf_op jit(solution)/shard_map/while/body/eval_jaxpr/dot_general | solution.py:57
  330.0 0.7 dynamic-slice_bitcast_fusion.2
  330.8 8.7 %fusion.83 = f32[9,512]{1,0:T(8,128)S(1)} fusion(f32[9,4096]{1,0:T(8,128)} %get-tuple-element.305, f32[512]{0:T(512)S(1)} %get-tuple-element.247, f32[4096]{0:T(1024)S(1)} %bitcast.94, f32[512]{0:T(512)S(1)} %get-tuple-element.249, f32[4096]{0:T(1024)S(1)} %bitcast.95, f32[512]{0:T(512)S(1)} %get-tuple-element.251, f32[4096]{0:T(1024)S(1)} %bitcast.93, ...), kind=kOutput, calls=%fused_computation.26.clone.1 | convolution fusion | flops 251658240 | bytes 223232 | tf_op jit(solution)/shard_map/while/body/eval_jaxpr/dot_general | solution.py:57
  339.7 0.7 dynamic-slice_bitcast_fusion.2
  340.4 8.7 %fusion.83 = f32[9,512]{1,0:T(8,128)S(1)} fusion(f32[9,4096]{1,0:T(8,128)} %get-tuple-element.305, f32[512]{0:T(512)S(1)} %get-tuple-element.247, f32[4096]{0:T(1024)S(1)} %bitcast.94, f32[512]{0:T(512)S(1)} %get-tuple-element.249, f32[4096]{0:T(1024)S(1)} %bitcast.95, f32[512]{0:T(512)S(1)} %get-tuple-element.251, f32[4096]{0:T(1024)S(1)} %bitcast.93, ...), kind=kOutput, calls=%fused_computation.26.clone.1 | convolution fusion | flops 251658240 | bytes 223232 | tf_op jit(solution)/shard_map/while/body/eval_jaxpr/dot_general | solution.py:57
  349.3 0.7 dynamic-slice_bitcast_fusion.2
  350.1 8.7 %fusion.83 = f32[9,512]{1,0:T(8,128)S(1)} fusion(f32[9,4096]{1,0:T(8,128)} %get-tuple-element.305, f32[512]{0:T(512)S(1)} %get-tuple-element.247, f32[4096]{0:T(1024)S(1)} %bitcast.94, f32[512]{0:T(512)S(1)} %get-tuple-element.249, f32[4096]{0:T(1024)S(1)} %bitcast.95, f32[512]{0:T(512)S(1)} %get-tuple-element.251, f32[4096]{0:T(1024)S(1)} %bitcast.93, ...), kind=kOutput, calls=%fused_computation.26.clone.1 | convolution fusion | flops 251658240 | bytes 223232 | tf_op jit(solution)/shard_map/while/body/eval_jaxpr/dot_general | solution.py:57
  359.0 0.7 dynamic-slice_bitcast_fusion.2
  359.7 8.7 %fusion.83 = f32[9,512]{1,0:T(8,128)S(1)} fusion(f32[9,4096]{1,0:T(8,128)} %get-tuple-element.305, f32[512]{0:T(512)S(1)} %get-tuple-element.247, f32[4096]{0:T(1024)S(1)} %bitcast.94, f32[512]{0:T(512)S(1)} %get-tuple-element.249, f32[4096]{0:T(1024)S(1)} %bitcast.95, f32[512]{0:T(512)S(1)} %get-tuple-element.251, f32[4096]{0:T(1024)S(1)} %bitcast.93, ...), kind=kOutput, calls=%fused_computation.26.clone.1 | convolution fusion | flops 251658240 | bytes 223232 | tf_op jit(solution)/shard_map/while/body/eval_jaxpr/dot_general | solution.py:57
  368.6 0.7 dynamic-slice_bitcast_fusion.2
  369.4 8.7 %fusion.83 = f32[9,512]{1,0:T(8,128)S(1)} fusion(f32[9,4096]{1,0:T(8,128)} %get-tuple-element.305, f32[512]{0:T(512)S(1)} %get-tuple-element.247, f32[4096]{0:T(1024)S(1)} %bitcast.94, f32[512]{0:T(512)S(1)} %get-tuple-element.249, f32[4096]{0:T(1024)S(1)} %bitcast.95, f32[512]{0:T(512)S(1)} %get-tuple-element.251, f32[4096]{0:T(1024)S(1)} %bitcast.93, ...), kind=kOutput, calls=%fused_computation.26.clone.1 | convolution fusion | flops 251658240 | bytes 223232 | tf_op jit(solution)/shard_map/while/body/eval_jaxpr/dot_general | solution.py:57
  378.3 0.7 dynamic-slice_bitcast_fusion.2
  379.0 8.7 %fusion.83 = f32[9,512]{1,0:T(8,128)S(1)} fusion(f32[9,4096]{1,0:T(8,128)} %get-tuple-element.305, f32[512]{0:T(512)S(1)} %get-tuple-element.247, f32[4096]{0:T(1024)S(1)} %bitcast.94, f32[512]{0:T(512)S(1)} %get-tuple-element.249, f32[4096]{0:T(1024)S(1)} %bitcast.95, f32[512]{0:T(512)S(1)} %get-tuple-element.251, f32[4096]{0:T(1024)S(1)} %bitcast.93, ...), kind=kOutput, calls=%fused_computation.26.clone.1 | convolution fusion | flops 251658240 | bytes 223232 | tf_op jit(solution)/shard_map/while/body/eval_jaxpr/dot_general | solution.py:57
  387.9 0.7 dynamic-slice_bitcast_fusion.2
  388.7 8.7 %fusion.83 = f32[9,512]{1,0:T(8,128)S(1)} fusion(f32[9,4096]{1,0:T(8,128)} %get-tuple-element.305, f32[512]{0:T(512)S(1)} %get-tuple-element.247, f32[4096]{0:T(1024)S(1)} %bitcast.94, f32[512]{0:T(512)S(1)} %get-tuple-element.249, f32[4096]{0:T(1024)S(1)} %bitcast.95, f32[512]{0:T(512)S(1)} %get-tuple-element.251, f32[4096]{0:T(1024)S(1)} %bitcast.93, ...), kind=kOutput, calls=%fused_computation.26.clone.1 | convolution fusion | flops 251658240 | bytes 223232 | tf_op jit(solution)/shard_map/while/body/eval_jaxpr/dot_general | solution.py:57
  397.5 1.4 add.106
  (96 shorter events, 2.3 us)
Async XLA Ops:
  7.4 28.0 %all-gather.2.cloned.1.call-start = ((), (), s32[]{:S(2)}) async-start(), calls=%async_computation.1 | async-start | bytes 1327104 | tf_op jit(solution)/shard_map/all_gather | solution.py:77
  11.2 309.1 %all-reduce.2.cloned.1.call-start = ((), (), s32[]{:S(2)}) async-start(), calls=%async_computation.3 | async-start | bytes 524288 | tf_op jit(solution)/shard_map/psum | solution.py:108
  35.4 30.8 %collective-permute-start.1 = (f32[256,9,128]{2,0,1:T(8,128)}, f32[256,9,128]{2,0,1:T(8,128)S(1)}, u32[]{:S(2)}, u32[]{:S(2)}) collective-permute-start(f32[256,9,128]{2,0,1:T(8,128)} %all-gather.2.cloned.1.call-done), channel_id=1, source_target_pairs={{8,0},{16,8},{24,16},{32,24},{40,32},{48,40},{56,48},{64,56},{72,6... | collective-permute-start | bytes 3538952 | tf_op jit(solution)/shard_map/ppermute | solution.py:23
  40.2 31.4 %collective-permute-start = (f32[256,9,128]{2,0,1:T(8,128)}, f32[256,9,128]{2,0,1:T(8,128)S(1)}, u32[]{:S(2)}, u32[]{:S(2)}) collective-permute-start(f32[256,9,128]{2,0,1:T(8,128)} %all-gather.2.cloned.1.call-done), channel_id=1, source_target_pairs={{0,8},{8,16},{16,24},{24,32},{32,40},{40,48},{48,56},{56,64},{64,7... | collective-permute-start | bytes 3538952 | tf_op jit(solution)/shard_map/ppermute | solution.py:22
  103.0 71.5 %copy-start.1 = (s32[32]{0:T(128)S(1)}, s32[32]{0:T(128)}, u32[]{:S(2)}) copy-start(s32[32]{0:T(128)} %param.10) | copy-start | bytes 388
  103.0 217.3 %copy-start = (f32[3,4096]{1,0:T(4,128)S(1)}, f32[3,4096]{1,0:T(4,128)}, u32[]{:S(2)}) copy-start(f32[3,4096]{1,0:T(4,128)} %param.11) | copy-start | bytes 147460
  103.2 76.6 %collective-permute-start.2 = (f32[256,3,128]{2,0,1:T(8,128)S(1)}, f32[256,3,128]{2,0,1:T(8,128)S(1)}, u32[]{:S(2)}, u32[]{:S(2)}) collective-permute-start(f32[256,3,128]{2,0,1:T(8,128)S(1)} %get-tuple-element.141), channel_id=1, source_target_pairs={{0,120},{8,0},{16,8},{24,16},{32,24},{40,32},{48,40},{56,48},{64,5... | collective-permute-start | bytes 1179656 | tf_op jit(solution)/shard_map/ppermute | solution.py:30
  103.5 78.3 %collective-permute-start.3 = (f32[256,3,128]{2,0,1:T(8,128)S(1)}, f32[256,3,128]{2,0,1:T(8,128)S(1)}, u32[]{:S(2)}, u32[]{:S(2)}) collective-permute-start(f32[256,3,128]{2,0,1:T(8,128)S(1)} %get-tuple-element.142), channel_id=1, source_target_pairs={{0,8},{8,16},{16,24},{24,32},{32,40},{40,48},{48,56},{56,64},{64,7... | collective-permute-start | bytes 1179656 | tf_op jit(solution)/shard_map/ppermute | solution.py:30
  175.6 221.8 %reduce-scatter.2.cloned.1.call-start = ((), (), s32[]{:S(2)}) async-start(), calls=%async_computation.2 | async-start | bytes 442368 | tf_op jit(solution)/shard_map/reduce_scatter | solution.py:103
Sparse Core Ops, SparseCore 0:
  11.3 24.0 all-gather.1
  182.7 33.0 reduce-scatter.1
Sparse Core Ops, SparseCore 1:
  175.7 144.5 all-reduce.1
where the time goes:
time: 410 us; the launch traced here: 406 us
  waiting for transfers between devices  198 us (48%)
  matrix products  79.7 us (19%)
  starting transfers between devices  76.1 us (19%)
  local copies, waits for them, and re-layouts  20 us (5%)
  other arithmetic  16.6 us (4%)
  between operations  15.6 us (4%)
    psum x1, waiting for transfers between devices, on_device(): moments = lax.psum(local_moments, ('space', 'sub'))  138 us
    ppermute x2, starting transfers between devices, from_behind(): lax.ppermute(shard, axis, [(i, (i + by) % devices) for i in range(devices)])  70.9 us
    dot_general x8, matrix products, far_group(): grid = jnp.dot(moments, weight, precision=highest)  69.5 us
    ppermute x1, waiting for transfers between devices, with_halo(): after = lax.ppermute(initial, axis, down)  24.5 us
    all_gather x1, waiting for transfers between devices, on_device(): gathered = lax.all_gather(packed, 'sub', axis=0, tiled=True)  24.2 us
  transfers between devices with their start and end apart: 7, of which 6 were waited for; matrix products, arithmetic and copies ran while one was open for 20% of the time, Pallas kernels for 0%

commit v1 on v0

v1 whole, which is shorter than its diff:
```python
import functools

import jax
import jax.numpy as jnp
from jax import lax
from jax.experimental import pallas as pl
from jax.experimental.pallas import tpu as pltpu
from jax.sharding import PartitionSpec as P

MESH = pl.DeviceIdType.MESH
f32 = jnp.float32
bf16 = jnp.bfloat16
ROWS = 296
UNROLL = 4
SEG_TILE = 2048


def three(x):
    a = x.astype(bf16).astype(f32)
    r = x - a
    b = r.astype(bf16).astype(f32)
    return a, b, (r - b).astype(bf16).astype(f32)


def exchange_and_far(
    seg_ref, cell_ref, cc_ref, pair_ref, far_ref, win_ref,
    payload, flat, mine, parts, moments, cells_f, segs_f, acc,
    x_send, w_send, r_send, w_recv, p_send, p_recv, m_send, m_recv, own_sem,
):
    space = lax.axis_index("space")
    sub = lax.axis_index("sub")
    z, core = sub // 2, sub % 2
    nblocks = seg_ref.shape[0]
    ncell = cc_ref.shape[1]
    per = ncell // 16

    barrier = pltpu.get_barrier_semaphore()

    def greet_sub(k, c):
        pl.semaphore_signal(
            barrier, inc=1, device_id=(space, (sub + k) % 8), device_id_type=MESH
        )
        return c

    def greet_space(k, c):
        pl.semaphore_signal(
            barrier, inc=1, device_id=((space + k) % 16, sub), device_id_type=MESH
        )
        return c

    lax.fori_loop(1, 8, greet_sub, 0)
    lax.fori_loop(1, 16, greet_space, 0)

    base = space * per
    own_cc = cc_ref[:, pl.ds(pl.multiple_of(base, 256), per)]
    hot = (
        cell_ref[...] - base == lax.broadcasted_iota(jnp.int32, (nblocks, per), 1)
    ).astype(f32)
    centre = lax.dot_general(
        own_cc, hot, (((1,), (1,)), ((), ())),
        precision=lax.Precision.HIGHEST, preferred_element_type=f32,
    )
    origin = centre[:, 0:1]
    total = jnp.zeros((9, per), f32)
    for g in range(nblocks):
        lanes = slice(g * 128, g * 128 + 128)
        pos = seg_ref[g, 0:3, :] + centre[:, g : g + 1]
        rest = seg_ref[g, 3:9, :]
        payload[9 * g : 9 * g + 3, :] = pos
        payload[9 * g + 3 : 9 * g + 9, :] = rest
        flat[0:3, lanes] = pos
        flat[8:11, lanes] = rest[0:3]
        line, burg = rest[0:3], rest[3:6]
        outer = jnp.concatenate([burg[a : a + 1] * line for a in range(3)], axis=0)
        total = total + jnp.sum(outer, axis=1, keepdims=True) * hot[g : g + 1, :]
    payload[288:296, :] = pair_ref[...]
    mine[0:9, :] = total
    mine[9:16, :] = jnp.zeros((7, per), f32)

    pl.semaphore_wait(barrier, 22)

    def part_copy(k):
        to = (sub + k) % 8
        return pltpu.make_async_remote_copy(
            src_ref=mine, dst_ref=parts.at[7 - k],
            send_sem=p_send.at[k - 1], recv_sem=p_recv.at[7 - k],
            device_id=(space, to), device_id_type=MESH,
        )


    def start_part(k, c):
        part_copy(k).start()
        return c

    lax.fori_loop(1, 8, start_part, 0)

    def beside(step, slot, sem):
        return pltpu.make_async_remote_copy(
            src_ref=payload, dst_ref=win_ref.at[slot, sub],
            send_sem=x_send.at[sem], recv_sem=w_recv.at[slot, sub],
            device_id=((space + step) % 16, sub), device_id_type=MESH,
        )

    right, left = beside(1, 0, 0), beside(15, 2, 1)
    right.start()
    left.start()
    own_copy = pltpu.make_async_copy(payload, win_ref.at[1, sub], own_sem)
    own_copy.start()

    def spread(slot, k):
        src = payload if slot == 1 else win_ref.at[slot, sub]
        if k == 0:
            to = z * 2 + 1 - core
        else:
            to = (z + k) % 4 * 2 + core
        return pltpu.make_async_remote_copy(
            src_ref=src, dst_ref=win_ref.at[slot, sub],
            send_sem=w_send.at[slot, k], recv_sem=w_recv.at[slot, sub],
            device_id=(space, to), device_id_type=MESH,
        )

    def arrived(slot, place):
        pltpu.make_async_copy(
            win_ref.at[slot, place], win_ref.at[slot, place], w_recv.at[slot, place]
        ).wait()

    def relay(slot, k):
        place = (z + k) % 4 * 2 + core
        return pltpu.make_async_remote_copy(
            src_ref=win_ref.at[slot, place], dst_ref=win_ref.at[slot, place],
            send_sem=r_send.at[slot, k - 1], recv_sem=w_recv.at[slot, place],
            device_id=(space, z * 2 + 1 - core), device_id_type=MESH,
        )

    for k in (1, 3, 2, 0):
        spread(1, k).start()

    ones = jnp.ones((3, ncell), f32)
    blank = jnp.zeros((8, ncell), f32)
    c = cc_ref[...] - origin
    c1, c2, c3 = three(c)
    cq = jnp.concatenate(three(jnp.sum(c * c, axis=0, keepdims=True)), axis=0)
    cells_f[...] = jnp.transpose(
        jnp.concatenate([c1, c1, c2, c2, c1, c3, cq, ones, blank], axis=0)
    ).astype(bf16)
    p = flat[0:3, :] - origin
    p1, p2, p3 = three(-2.0 * p)
    pq = jnp.concatenate(three(1.0 + jnp.sum(p * p, axis=0, keepdims=True)), axis=0)
    segs_f[...] = jnp.concatenate(
        [p1, p2, p1, p2, p3, p1, ones, pq, blank], axis=0
    ).astype(bf16)

    region = mine[...]
    for k in range(7):
        pltpu.make_async_copy(parts.at[k], parts.at[k], p_recv.at[k]).wait()
        region = region + parts[k]
    moments[0] = region

    def moment_copy(k):
        return pltpu.make_async_remote_copy(
            src_ref=moments.at[0], dst_ref=moments.at[16 - k],
            send_sem=m_send.at[k], recv_sem=m_recv.at[16 - k],
            device_id=((space + k) % 16, sub), device_id_type=MESH,
        )

    def start_moment(k, c):
        moment_copy(k).start()
        return c

    lax.fori_loop(1, 16, start_moment, 0)

    def split_moments(k):
        m = moments[k]
        hi = m.astype(bf16)
        return jnp.concatenate([hi, (m - hi.astype(f32)).astype(bf16)], axis=0)

    def far_chunk(k, first):
        at = pl.multiple_of((space + k) % 16 * per, 256)
        cells = cells_f[pl.ds(at, per), :]
        m = split_moments(k)
        cell_id = at + lax.broadcasted_iota(jnp.int32, (per, 128), 0)

        def tile(j, carry):
            lanes = pl.ds(pl.multiple_of(j * SEG_TILE, SEG_TILE), SEG_TILE)
            d = jnp.dot(cells, segs_f[:, lanes], preferred_element_type=f32)
            w = pl.reciprocal(d, approx=True)
            if first:
                cols = []
                for q in range(SEG_TILE // 128):
                    block = cell_ref[pl.ds(j * (SEG_TILE // 128) + q, 1), :]
                    cols.append(
                        jnp.where(cell_id == block, 0.0, w[:, q * 128 : q * 128 + 128])
                    )
                w = jnp.concatenate(cols, axis=1)
            hi = w.astype(bf16)
            lo = (w - hi.astype(f32)).astype(bf16)
            g = jnp.dot(m, hi, preferred_element_type=f32)
            g = g + jnp.dot(m, lo, preferred_element_type=f32)
            if first:
                acc[:, lanes] = g
            else:
                acc[:, lanes] += g
            return carry

        lax.fori_loop(0, nblocks * 128 // SEG_TILE, tile, 0)

    def later_chunk(k, carry):
        pltpu.make_async_copy(moments.at[k], moments.at[k], m_recv.at[k]).wait()
        far_chunk(k, False)
        return carry

    far_chunk(0, True)
    lax.fori_loop(1, 3, later_chunk, 0)
    arrived(0, sub)
    arrived(2, sub)
    for slot in (0, 2):
        for k in (1, 3, 2, 0):
            spread(slot, k).start()
    lax.fori_loop(3, 6, later_chunk, 0)
    for k in (1, 3, 2):
        arrived(1, (z + k) % 4 * 2 + core)
        relay(1, k).start()
    lax.fori_loop(6, 13, later_chunk, 0)
    for slot in (0, 2):
        for k in (1, 3, 2):
            arrived(slot, (z + k) % 4 * 2 + core)
            relay(slot, k).start()
    lax.fori_loop(13, 16, later_chunk, 0)

    grid = acc[0:9, :] + acc[16:25, :]
    line = flat[8:11, :]
    for a in range(3):
        row = jnp.sum(grid[3 * a : 3 * a + 3, :] * line, axis=0, keepdims=True)
        for g in range(nblocks):
            far_ref[g, a : a + 1, :] = row[:, g * 128 : g * 128 + 128]

    other = 1 - core
    for slot in range(3):
        for k in range(4):
            arrived(slot, (z + k) % 4 * 2 + other)
    own_copy.wait()
    right.wait_send()
    left.wait_send()
    for slot in range(3):
        for k in range(4):
            spread(slot, k).wait_send()
        for k in range(1, 4):
            relay(slot, k).wait_send()

    def end_part(k, c):
        part_copy(k).wait_send()
        return c

    def end_moment(k, c):
        moment_copy(k).wait_send()
        return c

    lax.fori_loop(1, 8, end_part, 0)
    lax.fori_loop(1, 16, end_moment, 0)


def near_kernel(win_ref, place_ref, far_ref, out_ref, feats, arrange, acc, listed, table, sem):
    space, sub = place_ref[0], place_ref[1]
    nblocks = far_ref.shape[0]
    first_block = ((space * 8 + sub) * nblocks).astype(f32)
    row_of = lambda dev, block: dev * ROWS + 9 * block
    my_row = (8 + sub) * ROWS
    row16 = lax.broadcasted_iota(jnp.int32, (16, 128), 0)

    target = jnp.concatenate(
        [win_ref[d * ROWS + 288 : d * ROWS + 289, :] for d in range(24)]
        + [win_ref[pl.ds(my_row + 288, 1), :]], axis=0
    )
    source = jnp.concatenate(
        [win_ref[d * ROWS + 289 : d * ROWS + 290, :] for d in range(24)]
        + [win_ref[pl.ds(my_row + 289, 1), :]], axis=0
    )
    item_row = lax.broadcasted_iota(jnp.int32, (25, 128), 0)
    is_own = item_row == 24
    mine = jnp.where(is_own, target, source) - first_block
    theirs = jnp.where(is_own, source, target)
    used = (source >= 0) & (mine >= 0) & (mine < nblocks)
    owner = jnp.floor(theirs * (1.0 / 32))
    their_space = jnp.floor(owner * (1.0 / 8))
    ahead = their_space - space.astype(f32) + 1.0
    ahead = jnp.where(ahead < 0, ahead + 16.0, jnp.where(ahead >= 16, ahead - 16.0, ahead))
    dev = ahead * 8.0 + (owner - 8.0 * their_space)
    local = theirs - 32.0 * owner
    usedf = used.astype(f32)
    before = (
        lax.broadcasted_iota(jnp.int32, (128, 128), 0)
        < lax.broadcasted_iota(jnp.int32, (128, 128), 1)
    ).astype(bf16)
    rank = jnp.dot(usedf.astype(bf16), before, preferred_element_type=f32)
    sums = jnp.sum(usedf, axis=1, keepdims=True)
    above = (
        lax.broadcasted_iota(jnp.int32, (25, 25), 1)
        < lax.broadcasted_iota(jnp.int32, (25, 25), 0)
    ).astype(f32)
    starts = jnp.dot(
        above, jnp.broadcast_to(sums, (25, 128)), precision=lax.Precision.HIGHEST,
        preferred_element_type=f32,
    )
    rank = jnp.where(used, rank + starts, -1.0)
    count = jnp.sum(usedf).astype(jnp.int32)
    pad = jnp.full((128 - 25, 128), -1.0, f32)
    rank_t = jnp.transpose(jnp.concatenate([rank, pad], axis=0))
    lane = lax.broadcasted_iota(jnp.int32, (128, 128), 1).astype(f32)
    row8 = lax.broadcasted_iota(jnp.int32, (8, 128), 0)

    def fill(kr, carry):
        got = jnp.zeros((8, 128), f32)
        want = lane + (kr * 128).astype(f32)
        for r in range(25):
            hot = (rank_t[:, r : r + 1] == want).astype(bf16)
            vals = jnp.where(
                row8 == 0, dev[r : r + 1], jnp.where(row8 == 1, local[r : r + 1], mine[r : r + 1])
            )
            vals = jnp.where(row8 < 3, vals, 0.0)
            vals = jnp.where(used[r : r + 1], vals, 0.0)
            got = got + jnp.dot(vals.astype(bf16), hot, preferred_element_type=f32)
        other = got[0:1] * float(ROWS) + got[1:2] * 9.0
        rows = jnp.where(row8 == 0, other, jnp.where(row8 == 1, got[2:3], 0.0))
        listed[...] = rows.astype(jnp.int32)
        copy = pltpu.make_async_copy(listed, table.at[pl.ds(kr * 8, 8)], sem)
        copy.start()
        copy.wait()
        return carry

    lax.fori_loop(0, (count + 127) // 128, fill, 0)

    origin_col = jnp.where(
        lax.broadcasted_iota(jnp.int32, (16, 1), 0) < 3, win_ref[pl.ds(my_row, 16), 0:1], 0.0
    )

    def split_rows(x, plus):
        x = x - origin_col
        a, b, c = three(x)
        sq = jnp.sum(jnp.where(row16 < 3, x * x, 0.0), axis=0, keepdims=True) + plus
        s1, s2, s3 = three(sq)
        ext = jnp.where(
            row16 < 3, 1.0,
            jnp.where(row16 == 3, s1, jnp.where(row16 == 4, s2, jnp.where(row16 == 5, s3, 0.0))),
        )
        return x, a.astype(bf16), b.astype(bf16), c.astype(bf16), ext.astype(bf16)

    r = lax.broadcasted_iota(jnp.int32, (64, 384), 0)
    q = lax.broadcasted_iota(jnp.int32, (64, 384), 1)
    kind, col = q // 128, q % 128
    group, line = col // 16, col % 16
    mate = jnp.where(group < 3, group, jnp.where(group < 5, group - 3, 0))
    dist = (kind == 0) & (group < 6) & (line < 3) & (r == mate * 16 + line)
    extra = (kind == 0) & (group == 6) & (
        ((line < 3) & (r == 48 + 3 + line)) | ((line >= 3) & (line < 6) & (r == 48))
    )
    burg_line = (kind == 1) & (group < 6) & (line >= 3) & (line < 6) & (r == mate * 16 + line + 3)
    line_burg = (kind == 2) & (group < 6) & (line >= 6) & (line < 9) & (r == mate * 16 + line - 3)
    arrange[...] = jnp.where(
        dist, -2.0, jnp.where(extra | burg_line | line_burg, 1.0, 0.0)
    ).astype(bf16)

    def own_features(g, carry):
        _, a, b, c, ext = split_rows(win_ref[pl.ds(my_row + 9 * g, 16), :], 0.25)
        x = jnp.concatenate([a, b, c, ext], axis=0)
        f = lax.dot_general(
            x, arrange[...], (((0,), (0,)), ((), ())), preferred_element_type=f32
        )
        for kind in range(3):
            feats[g, kind * 128 : kind * 128 + 128, :] = f[
                :, kind * 128 : kind * 128 + 128
            ].astype(bf16)
        acc[g] = jnp.zeros((128, 128), f32)
        return carry

    lax.fori_loop(0, nblocks, own_features, 0)

    def items(step, carry):
        work = []
        for u in range(UNROLL):
            k = step * UNROLL + u
            kk = jnp.minimum(k, count - 1)
            alive = (k < count).astype(f32)
            other = table[kk // 128 * 8, kk % 128]
            own = table[kk // 128 * 8 + 1, kk % 128]
            _, a, b, c, ext = split_rows(win_ref[pl.ds(other, 16), :], 0.0)
            rhs = jnp.concatenate([a, a, a, b, b, c, ext, jnp.zeros((16, 128), bf16)], axis=0)
            work.append((own, alive, rhs))
        outs = []
        for own, alive, rhs in work:
            outs.append(jnp.dot(feats[own], rhs, preferred_element_type=f32))
        for (own, alive, rhs), out in zip(work, outs):
            inv = lax.rsqrt(jnp.maximum(out[0:128], 0.25))
            g = (inv * inv) * (inv * alive) * (out[128:256] * out[256:384])
            hi = g.astype(bf16)
            lo = (g - hi.astype(f32)).astype(bf16)
            both = lax.dot_general(
                jnp.concatenate([hi, lo], axis=0), rhs, (((1,), (1,)), ((), ())),
                preferred_element_type=f32,
            )
            acc[own] += both[0:128] + both[128:256]
        return carry

    lax.fori_loop(0, (count + UNROLL - 1) // UNROLL, items, 0)

    def finish(g, carry):
        t = jnp.transpose(acc[g])
        p = win_ref[pl.ds(my_row + 9 * g, 16), :] - origin_col
        gp = t[0:3] + t[48:51] + t[80:83]
        out_ref[g] = far_ref[g] + p[0:3] * t[96:97] - gp
        return carry

    lax.fori_loop(0, nblocks, finish, 0)


def on_device(seg_data, cell_of_block, cell_center, pairs, live_count):
    nblocks, _, width = seg_data.shape
    ncell = cell_center.shape[1]
    slots = pairs.shape[0]
    live = jnp.arange(slots, dtype=jnp.int32)[None, :] < live_count
    pair_rows = jnp.where(live, pairs.T, -1).astype(f32)
    pair_rows = jnp.concatenate([pair_rows, jnp.zeros((6, slots), f32)], axis=0)
    vmem = pl.BlockSpec(memory_space=pltpu.VMEM)
    dma = pltpu.SemaphoreType.DMA
    far, window = pl.pallas_call(
        exchange_and_far,
        out_shape=(
            jax.ShapeDtypeStruct((nblocks, 3, width), f32),
            jax.ShapeDtypeStruct((3, 8, ROWS, width), f32),
        ),
        in_specs=[vmem] * 4,
        out_specs=(vmem, pl.BlockSpec(memory_space=pl.ANY)),
        scratch_shapes=[
            pltpu.VMEM((ROWS, width), f32),
            pltpu.VMEM((16, nblocks * width), f32),
            pltpu.VMEM((16, ncell // 16), f32),
            pltpu.VMEM((7, 16, ncell // 16), f32),
            pltpu.VMEM((16, 16, ncell // 16), f32),
            pltpu.VMEM((ncell, 32), bf16),
            pltpu.VMEM((32, nblocks * width), bf16),
            pltpu.VMEM((32, nblocks * width), f32),
            dma((2,)), dma((3, 4)), dma((3, 3)), dma((3, 8)),
            dma((7,)), dma((7,)), dma((16,)), dma((16,)), dma,
        ],
        compiler_params=pltpu.CompilerParams(
            collective_id=0, has_side_effects=True, vmem_limit_bytes=48 << 20
        ),
    )(seg_data, cell_of_block[:, None], cell_center, pair_rows)
    place = jnp.stack([lax.axis_index("space"), lax.axis_index("sub")]).astype(jnp.int32)
    return pl.pallas_call(
        near_kernel,
        out_shape=jax.ShapeDtypeStruct((nblocks, 3, width), f32),
        in_specs=[vmem, pl.BlockSpec(memory_space=pltpu.SMEM), vmem],
        out_specs=vmem,
        scratch_shapes=[
            pltpu.VMEM((nblocks, 384, width), bf16),
            pltpu.VMEM((64, 384), bf16),
            pltpu.VMEM((nblocks, width, width), f32),
            pltpu.VMEM((8, width), jnp.int32),
            pltpu.SMEM((25 * 8, width), jnp.int32),
            pltpu.SemaphoreType.DMA,
        ],
        compiler_params=pltpu.CompilerParams(vmem_limit_bytes=48 << 20),
    )(window.reshape(24 * ROWS, width), place, far)


def solution(mesh):
    placed = (
        P(("space", "sub"), None, None),
        P(("space", "sub")),
        P(),
        P(("space", "sub"), None),
        P(("space", "sub")),
    )
    return jax.shard_map(
        on_device,
        mesh=mesh,
        in_specs=placed,
        out_specs=P(("space", "sub"), None, None),
        check_vma=False,
    )
```

time: 410 us -> 86.7 us (0.21)
  the two profiles are of different devices: /device:TPU:32 before, /device:TPU:33 now
where the time goes in v1:
time: 86.7 us; the launch traced here: 86.5 us
  Pallas kernels  78 us (90%)
  local copies, waits for them, and re-layouts  7.01 us (8%)
    pallas_call x1, Pallas kernels, on_device(): pl.pallas_call(near_kernel, out_shape=jax.ShapeDtypeStruct((nblocks, 3, w...  39.1 us
    pallas_call x1, Pallas kernels, on_device(): pl.pallas_call(exchange_and_far, out_shape=(jax.ShapeDtypeStruct((nblocks...  38.9 us
    unnamed x7, local copies, waits for them, and re-layouts  5.64 us

profile of v1, /device:TPU:33, one launch (start us, length us, event | category | flops | bytes accessed | tf_op | source)
XLA Modules:
  0.0 86.5 jit_solution(12521033699700036271)
XLA Ops:
  0.0 1.0 %copy.6.seg_ref = f32[32,9,128]{2,1,0:T(8,128)S(1)} copy(f32[32,9,128]{2,0,1:T(8,128)} %param.5) | data formatting | bytes 294912 | tf_op args[0]
  1.0 0.7 copy.7.cell_ref
  2.4 0.7 convert_bitcast_fusion
  3.1 0.0 copy-start.2
  3.1 0.8 copy-done.2
  3.9 38.9 %shard_map.55 = (f32[32,3,128]{2,1,0:T(4,128)S(1)}, f32[3,8,296,128]{3,2,1,0:T(8,128)S(1)}) custom-call(f32[32,9,128]{2,1,0:T(8,128)S(1)} %copy.6.seg_ref, s32[32,1]{1,0:T(8,128)S(1)} %copy.7.cell_ref, f32[3,4096]{1,0:T(4,128)S(1)} %copy-done.2, f32[8,128]{1,0:T(8,128)S(1)} %concatenate.3.pair_ref), custom_call_target="tpu_custom_call" | custom-call | tf_op jit(solution)/shard_map/pallas_call | solution.py:424
  42.9 0.0 copy-start
  42.9 1.8 %copy-done = f32[3,8,296,128]{3,2,1,0:T(8,128)} copy-done((f32[3,8,296,128]{3,2,1,0:T(8,128)}, f32[3,8,296,128]{3,2,1,0:T(8,128)S(1)}, u32[]{:S(2)}) %copy-start) | copy-done | bytes 3637272
  44.7 0.1 pad_add_fusion.place_ref
  44.7 0.0 copy-start.1
  44.7 2.0 %copy-done.1 = f32[3,8,296,128]{3,2,1,0:T(8,128)S(1)} copy-done((f32[3,8,296,128]{3,2,1,0:T(8,128)S(1)}, f32[3,8,296,128]{3,2,1,0:T(8,128)}, u32[]{:S(2)}) %copy-start.1) | copy-done | bytes 3637272
  46.8 39.1 %shard_map.56 = f32[32,3,128]{2,1,0:T(4,128)S(1)} custom-call(f32[7104,128]{1,0:T(8,128)S(1)} %bitcast.8, s32[2]{0:T(128)S(1)} %pad_add_fusion.place_ref, f32[32,3,128]{2,1,0:T(4,128)S(1)} %get-tuple-element.8.far_ref), custom_call_target="tpu_custom_call" | custom-call | tf_op jit(solution)/shard_map/pallas_call | solution.py:449
  85.9 0.6 copy.8
  (2 shorter events, 0.0 us)
Async XLA Ops:
  3.1 0.8 copy-start.2
  42.9 1.8 %copy-start = (f32[3,8,296,128]{3,2,1,0:T(8,128)}, f32[3,8,296,128]{3,2,1,0:T(8,128)S(1)}, u32[]{:S(2)}) copy-start(f32[3,8,296,128]{3,2,1,0:T(8,128)S(1)} %get-tuple-element.7) | copy-start | bytes 10911748
  44.7 2.0 %copy-start.1 = (f32[3,8,296,128]{3,2,1,0:T(8,128)S(1)}, f32[3,8,296,128]{3,2,1,0:T(8,128)}, u32[]{:S(2)}) copy-start(f32[3,8,296,128]{3,2,1,0:T(8,128)} %copy-done) | copy-start | bytes 10911748

commit v2 on v1

v2 whole, which is shorter than its diff:
```python
import functools

import jax
import jax.numpy as jnp
from jax import lax
from jax.experimental import pallas as pl
from jax.experimental.pallas import tpu as pltpu
from jax.sharding import PartitionSpec as P

MESH = pl.DeviceIdType.MESH
f32 = jnp.float32
bf16 = jnp.bfloat16
ROWS = 296
UNROLL = 8
SEG_TILE = 2048


def three(x):
    a = x.astype(bf16).astype(f32)
    r = x - a
    b = r.astype(bf16).astype(f32)
    return a, b, (r - b).astype(bf16).astype(f32)


def exchange_and_far(
    seg_hbm, cell_hbm, cc_hbm, pair_hbm, live_hbm, far_ref, win_ref,
    seg_ref, cell_row, cc_ref, pair_ref, live_ref, cell_ref,
    payload, flat, mine, parts, moments, cells_f, segs_f, acc,
    in_sem, x_send, w_send, r_send, w_recv, p_send, p_recv, m_send, m_recv, own_sem,
):
    space = lax.axis_index("space")
    sub = lax.axis_index("sub")
    z, core = sub // 2, sub % 2
    nblocks = seg_ref.shape[1]
    ncell = cc_ref.shape[1]
    per = ncell // 16

    ins = [
        pltpu.make_async_copy(src, dst, in_sem.at[i])
        for i, (src, dst) in enumerate(
            [
                (cell_hbm, cell_row), (cc_hbm, cc_ref), (seg_hbm, seg_ref),
                (pair_hbm, pair_ref), (live_hbm, live_ref),
            ]
        )
    ]
    for copy in ins:
        copy.start()
    barrier = pltpu.get_barrier_semaphore()

    def greet_sub(k, c):
        pl.semaphore_signal(
            barrier, inc=1, device_id=(space, (sub + k) % 8), device_id_type=MESH
        )
        return c

    def greet_space(k, c):
        pl.semaphore_signal(
            barrier, inc=1, device_id=((space + k) % 16, sub), device_id_type=MESH
        )
        return c

    lax.fori_loop(1, 8, greet_sub, 0)
    lax.fori_loop(1, 16, greet_space, 0)

    for copy in ins:
        copy.wait()

    base = space * per
    own_cc = cc_ref[:, pl.ds(pl.multiple_of(base, 256), per)]
    square = lax.broadcasted_iota(jnp.int32, (nblocks, nblocks), 0)
    lane = lax.broadcasted_iota(jnp.int32, (nblocks, nblocks), 1)
    cell = jnp.sum(
        jnp.where(square == lane, cell_row[...].astype(f32), 0.0), axis=1, keepdims=True
    )
    cell_ref[...] = jnp.broadcast_to(cell, (nblocks, 128)).astype(jnp.int32)
    hot = (
        cell.astype(jnp.int32) - base
        == lax.broadcasted_iota(jnp.int32, (nblocks, per), 1)
    ).astype(f32)
    origin = []
    for a in range(3):
        centre = jnp.sum(hot * own_cc[a : a + 1], axis=1, keepdims=True)
        origin.append(centre[0:1])
        payload[pl.ds(a, nblocks, stride=9), :] = seg_ref[a] + centre
    for a in range(3, 9):
        payload[pl.ds(a, nblocks, stride=9), :] = seg_ref[a]
    alive = lax.broadcasted_iota(jnp.int32, (2, 128), 1) < live_ref[...]
    payload[288:290, :] = jnp.where(alive, pair_ref[...].astype(f32), -1.0)
    payload[290:296, :] = jnp.zeros((6, 128), f32)
    for a in range(3):
        for b in range(3):
            outer = jnp.sum(seg_ref[6 + a] * seg_ref[3 + b], axis=1, keepdims=True)
            mine[3 * a + b : 3 * a + b + 1, :] = jnp.sum(hot * outer, axis=0, keepdims=True)
    mine[9:16, :] = jnp.zeros((7, per), f32)

    pl.semaphore_wait(barrier, 22)

    def part_copy(k):
        to = (sub + k) % 8
        return pltpu.make_async_remote_copy(
            src_ref=mine, dst_ref=parts.at[7 - k],
            send_sem=p_send.at[k - 1], recv_sem=p_recv.at[7 - k],
            device_id=(space, to), device_id_type=MESH,
        )


    def start_part(k, c):
        part_copy(k).start()
        return c

    lax.fori_loop(1, 8, start_part, 0)

    def beside(step, slot, sem):
        return pltpu.make_async_remote_copy(
            src_ref=payload, dst_ref=win_ref.at[slot, sub],
            send_sem=x_send.at[sem], recv_sem=w_recv.at[slot, sub],
            device_id=((space + step) % 16, sub), device_id_type=MESH,
        )

    right, left = beside(1, 0, 0), beside(15, 2, 1)
    right.start()
    left.start()
    own_copy = pltpu.make_async_copy(payload, win_ref.at[1, sub], own_sem)
    own_copy.start()

    def spread(slot, k):
        src = payload if slot == 1 else win_ref.at[slot, sub]
        if k == 0:
            to = z * 2 + 1 - core
        else:
            to = (z + k) % 4 * 2 + core
        return pltpu.make_async_remote_copy(
            src_ref=src, dst_ref=win_ref.at[slot, sub],
            send_sem=w_send.at[slot, k], recv_sem=w_recv.at[slot, sub],
            device_id=(space, to), device_id_type=MESH,
        )

    def arrived(slot, place):
        pltpu.make_async_copy(
            win_ref.at[slot, place], win_ref.at[slot, place], w_recv.at[slot, place]
        ).wait()

    def relay(slot, k):
        place = (z + k) % 4 * 2 + core
        return pltpu.make_async_remote_copy(
            src_ref=win_ref.at[slot, place], dst_ref=win_ref.at[slot, place],
            send_sem=r_send.at[slot, k - 1], recv_sem=w_recv.at[slot, place],
            device_id=(space, z * 2 + 1 - core), device_id_type=MESH,
        )

    for k in (1, 3, 2, 0):
        spread(1, k).start()

    for g in range(nblocks):
        lanes = slice(g * 128, g * 128 + 128)
        flat[0:3, lanes] = payload[9 * g : 9 * g + 3, :]
        flat[8:11, lanes] = payload[9 * g + 3 : 9 * g + 6, :]
    row3 = lax.broadcasted_iota(jnp.int32, (3, 1), 0)
    origin = jnp.where(row3 == 0, origin[0], jnp.where(row3 == 1, origin[1], origin[2]))
    ones = jnp.ones((3, ncell), f32)
    blank = jnp.zeros((8, ncell), f32)
    c = cc_ref[...] - origin
    c1, c2, c3 = three(c)
    cq = jnp.concatenate(three(jnp.sum(c * c, axis=0, keepdims=True)), axis=0)
    cells_f[...] = jnp.transpose(
        jnp.concatenate([c1, c1, c2, c2, c1, c3, cq, ones, blank], axis=0)
    ).astype(bf16)
    p = flat[0:3, :] - origin
    p1, p2, p3 = three(-2.0 * p)
    pq = jnp.concatenate(three(1.0 + jnp.sum(p * p, axis=0, keepdims=True)), axis=0)
    segs_f[...] = jnp.concatenate(
        [p1, p2, p1, p2, p3, p1, ones, pq, blank], axis=0
    ).astype(bf16)

    region = mine[...]
    for k in range(7):
        pltpu.make_async_copy(parts.at[k], parts.at[k], p_recv.at[k]).wait()
        region = region + parts[k]
    moments[0] = region

    def moment_copy(k):
        return pltpu.make_async_remote_copy(
            src_ref=moments.at[0], dst_ref=moments.at[16 - k],
            send_sem=m_send.at[k], recv_sem=m_recv.at[16 - k],
            device_id=((space + k) % 16, sub), device_id_type=MESH,
        )

    def start_moment(k, c):
        moment_copy(k).start()
        return c

    lax.fori_loop(1, 16, start_moment, 0)

    def split_moments(k):
        m = moments[k]
        hi = m.astype(bf16)
        return jnp.concatenate([hi, (m - hi.astype(f32)).astype(bf16)], axis=0)

    def far_chunk(k, first):
        at = pl.multiple_of((space + k) % 16 * per, 256)
        cells = cells_f[pl.ds(at, per), :]
        m = split_moments(k)
        cell_id = at + lax.broadcasted_iota(jnp.int32, (per, 128), 0)

        def tile(j, carry):
            lanes = pl.ds(pl.multiple_of(j * SEG_TILE, SEG_TILE), SEG_TILE)
            d = jnp.dot(cells, segs_f[:, lanes], preferred_element_type=f32)
            w = pl.reciprocal(d, approx=True)
            if first:
                cols = []
                for q in range(SEG_TILE // 128):
                    block = cell_ref[pl.ds(j * (SEG_TILE // 128) + q, 1), :]
                    cols.append(
                        jnp.where(cell_id == block, 0.0, w[:, q * 128 : q * 128 + 128])
                    )
                w = jnp.concatenate(cols, axis=1)
            hi = w.astype(bf16)
            lo = (w - hi.astype(f32)).astype(bf16)
            g = jnp.dot(m, hi, preferred_element_type=f32)
            g = g + jnp.dot(m, lo, preferred_element_type=f32)
            if first:
                acc[:, lanes] = g
            else:
                acc[:, lanes] += g
            return carry

        lax.fori_loop(0, nblocks * 128 // SEG_TILE, tile, 0)

    def later_chunk(k, carry):
        pltpu.make_async_copy(moments.at[k], moments.at[k], m_recv.at[k]).wait()
        far_chunk(k, False)
        return carry

    far_chunk(0, True)
    lax.fori_loop(1, 3, later_chunk, 0)
    arrived(0, sub)
    arrived(2, sub)
    for slot in (0, 2):
        for k in (1, 3, 2, 0):
            spread(slot, k).start()
    lax.fori_loop(3, 6, later_chunk, 0)
    for k in (1, 3, 2):
        arrived(1, (z + k) % 4 * 2 + core)
        relay(1, k).start()
    lax.fori_loop(6, 13, later_chunk, 0)
    for slot in (0, 2):
        for k in (1, 3, 2):
            arrived(slot, (z + k) % 4 * 2 + core)
            relay(slot, k).start()
    lax.fori_loop(13, 16, later_chunk, 0)

    grid = acc[0:9, :] + acc[16:25, :]
    line = flat[8:11, :]
    for a in range(3):
        far_ref[a : a + 1, :] = jnp.sum(
            grid[3 * a : 3 * a + 3, :] * line, axis=0, keepdims=True
        )

    other = 1 - core
    for slot in range(3):
        for k in range(4):
            arrived(slot, (z + k) % 4 * 2 + other)
    own_copy.wait()
    right.wait_send()
    left.wait_send()
    for slot in range(3):
        for k in range(4):
            spread(slot, k).wait_send()
        for k in range(1, 4):
            relay(slot, k).wait_send()

    def end_part(k, c):
        part_copy(k).wait_send()
        return c

    def end_moment(k, c):
        moment_copy(k).wait_send()
        return c

    lax.fori_loop(1, 8, end_part, 0)
    lax.fori_loop(1, 16, end_moment, 0)


def arrangement():
    r = lax.broadcasted_iota(jnp.int32, (64, 384), 0)
    q = lax.broadcasted_iota(jnp.int32, (64, 384), 1)
    kind, col = q // 128, q % 128
    group, line = col // 16, col % 16
    mate = jnp.where(group < 3, group, jnp.where(group < 5, group - 3, 0))
    dist = (kind == 0) & (group < 6) & (line < 3) & (r == mate * 16 + line)
    extra = (kind == 0) & (group == 6) & (
        ((line < 3) & (r == 48 + 3 + line)) | ((line >= 3) & (line < 6) & (r == 48))
    )
    burg_line = (kind == 1) & (group < 6) & (line >= 3) & (line < 6) & (r == mate * 16 + line + 3)
    line_burg = (kind == 2) & (group < 6) & (line >= 6) & (line < 9) & (r == mate * 16 + line - 3)
    return jnp.where(
        dist, -2.0, jnp.where(extra | burg_line | line_burg, 1.0, 0.0)
    ).astype(bf16)


def split_rows(x, plus):
    row16 = lax.broadcasted_iota(jnp.int32, (16, 128), 0)
    a, b, c = three(x)
    sq = jnp.sum(jnp.where(row16 < 3, x * x, 0.0), axis=0, keepdims=True) + plus
    s1, s2, s3 = three(sq)
    ext = jnp.where(
        row16 < 3, 1.0,
        jnp.where(row16 == 3, s1, jnp.where(row16 == 4, s2, jnp.where(row16 == 5, s3, 0.0))),
    )
    return a.astype(bf16), b.astype(bf16), c.astype(bf16), ext.astype(bf16)


def build_list(win_ref, space, sub, nblocks, hots, listed, table, sem):
    my_row = (8 + sub) * ROWS
    first_block = ((space * 8 + sub) * nblocks).astype(f32)
    target = jnp.concatenate(
        [win_ref[d * ROWS + 288 : d * ROWS + 289, :] for d in range(24)]
        + [win_ref[pl.ds(my_row + 288, 1), :]], axis=0
    )
    source = jnp.concatenate(
        [win_ref[d * ROWS + 289 : d * ROWS + 290, :] for d in range(24)]
        + [win_ref[pl.ds(my_row + 289, 1), :]], axis=0
    )
    is_own = lax.broadcasted_iota(jnp.int32, (25, 128), 0) == 24
    mine = jnp.where(is_own, target, source) - first_block
    theirs = jnp.where(is_own, source, target)
    used = (source >= 0) & (mine >= 0) & (mine < nblocks)
    mine = jnp.where(used, mine, -1.0)
    owner = jnp.floor(theirs * (1.0 / 32))
    their_space = jnp.floor(owner * (1.0 / 8))
    ahead = their_space - space.astype(f32) + 1.0
    ahead = jnp.where(ahead < 0, ahead + 16.0, jnp.where(ahead >= 16, ahead - 16.0, ahead))
    dev = ahead * 8.0 + (owner - 8.0 * their_space)
    local = theirs - 32.0 * owner
    before = (
        lax.broadcasted_iota(jnp.int32, (128, 128), 0)
        < lax.broadcasted_iota(jnp.int32, (128, 128), 1)
    ).astype(bf16)
    block_id = lax.broadcasted_iota(jnp.int32, (32, 128), 0).astype(f32)
    run = jnp.zeros((32, 1), f32)
    hots[...] = jnp.concatenate(
        [(mine[r : r + 1] == block_id).astype(f32) for r in range(25)], axis=0
    )
    within = jnp.dot(hots[...].astype(bf16), before, preferred_element_type=f32)
    sums = jnp.sum(hots[...], axis=1, keepdims=True)
    runs = []
    for r in range(25):
        runs.append(run)
        run = run + sums[32 * r : 32 * r + 32]
    even = 2.0 * jnp.floor((run + 1.0) * 0.5)
    above = (
        lax.broadcasted_iota(jnp.int32, (32, 32), 1)
        < lax.broadcasted_iota(jnp.int32, (32, 32), 0)
    ).astype(f32)
    starts = jnp.dot(
        above, jnp.broadcast_to(even, (32, 128)), precision=lax.Precision.HIGHEST,
        preferred_element_type=f32,
    )[:, 0:1]
    count = jnp.sum(even).astype(jnp.int32)
    ranks = []
    for r in range(25):
        h = hots[32 * r : 32 * r + 32, :]
        at = within[32 * r : 32 * r + 32] + (runs[r] + starts)
        ranks.append(jnp.sum(h * at, axis=0, keepdims=True))
    rank = jnp.where(used, jnp.concatenate(ranks, axis=0), -1.0)
    pad = jnp.full((128 - 25, 128), -1.0, f32)
    rank_t = jnp.transpose(jnp.concatenate([rank, pad], axis=0))
    lane = lax.broadcasted_iota(jnp.int32, (128, 128), 1).astype(f32)
    row8 = lax.broadcasted_iota(jnp.int32, (8, 128), 0)
    ends = starts + even

    def fill(kr, carry):
        got = jnp.zeros((8, 128), f32)
        first = (kr * 128).astype(f32)
        want = lane + first
        for r in range(25):
            hot = (rank_t[:, r : r + 1] == want).astype(bf16)
            vals = jnp.where(row8 == 0, dev[r : r + 1], jnp.where(row8 == 1, local[r : r + 1], 1.0))
            vals = jnp.where((row8 < 3) & used[r : r + 1], vals, 0.0)
            got = got + jnp.dot(vals.astype(bf16), hot, preferred_element_type=f32)
        other = got[0:1] * float(ROWS) + got[1:2] * 9.0
        own = jnp.sum((ends <= want[0:32]).astype(f32), axis=0, keepdims=True)
        own = jnp.minimum(own, 31.0)
        rows = jnp.where(
            row8 == 0, other, jnp.where(row8 == 1, own, jnp.where(row8 == 2, got[2:3], 0.0))
        )
        listed[...] = rows.astype(jnp.int32)
        copy = pltpu.make_async_copy(listed, table.at[pl.ds(kr * 8, 8)], sem)
        copy.start()
        copy.wait()
        return carry

    lax.fori_loop(0, (count + 127) // 128, fill, 0)
    return count


def near_kernel(win_ref, far_ref, out_ref, feats, arrange, acc, hots, listed, table, sem):
    space, sub = lax.axis_index("space"), lax.axis_index("sub")
    nblocks = out_ref.shape[1]
    my_row = (8 + sub) * ROWS
    origin = jnp.where(
        lax.broadcasted_iota(jnp.int32, (16, 1), 0) < 3, win_ref[pl.ds(my_row, 16), 0:1], 0.0
    )
    count = build_list(win_ref, space, sub, nblocks, hots, listed, table, sem)

    arrange[...] = arrangement()
    acc[...] = jnp.zeros_like(acc)
    for q in range(0, nblocks, 8):
        x = jnp.concatenate(
            [
                jnp.concatenate(
                    split_rows(win_ref[pl.ds(my_row + 9 * g, 16), :] - origin, 0.25), axis=0
                )
                for g in range(q, q + 8)
            ],
            axis=1,
        )
        f = lax.dot_general(
            x, arrange[...], (((0,), (0,)), ((), ())), preferred_element_type=f32
        )
        feats[q * 128 : q * 128 + 1024, :] = f.astype(bf16)

    half = lax.broadcasted_iota(jnp.int32, (1, 256), 1) < 128
    top = lax.broadcasted_iota(jnp.int32, (16, 128), 0) < 3

    def items(step, carry):
        work = []
        for u in range(UNROLL):
            k = (step * UNROLL + u) * 2
            inside = k < count
            k = jnp.minimum(k, count - 2)
            row = k // 128 * 8
            col = k % 128
            own = table[row + 1, col]
            rhs = []
            alive = []
            for v in range(2):
                other = table[row, col + v]
                alive.append(jnp.where(inside, table[row + 2, col + v], 0).astype(f32))
                a, b, c, ext = split_rows(win_ref[pl.ds(other, 16), :] - origin, 0.0)
                rhs.append(
                    jnp.concatenate(
                        [a, a, a, b, b, c, ext, jnp.zeros((16, 128), bf16)], axis=0
                    )
                )
            f = feats[pl.ds(pl.multiple_of(own * 128, 128), 128), :]
            f = jnp.concatenate([f[:, 0:128], f[:, 128:256], f[:, 256:384]], axis=0)
            work.append((own, jnp.where(half, alive[0], alive[1]), f, jnp.concatenate(rhs, axis=1)))
        outs = [jnp.dot(f, rhs, preferred_element_type=f32) for _, _, f, rhs in work]
        sums = []
        for (own, live, _, rhs), out in zip(work, outs):
            inv = lax.rsqrt(jnp.maximum(out[0:128], 0.25))
            g = (inv * inv) * (inv * live) * (out[128:256] * out[256:384])
            hi = g.astype(bf16)
            lo = (g - hi.astype(f32)).astype(bf16)
            lhs = jnp.concatenate([rhs[0:16], rhs[48:64], rhs[80:112]], axis=0)
            dims = (((1,), (1,)), ((), ()))
            r = lax.dot_general(lhs, hi, dims, preferred_element_type=f32)
            r = r + lax.dot_general(lhs, lo, dims, preferred_element_type=f32)
            sums.append((own, jnp.where(top, r[0:16] + r[16:32] + r[32:48], r[48:49])))
        for own, r in sums:
            acc[own] += r
        return carry

    lax.fori_loop(0, (count // 2 + UNROLL - 1) // UNROLL, items, 0)

    for g in range(nblocks):
        p = win_ref[pl.ds(my_row + 9 * g, 16), :] - origin
        t = acc[g]
        force = far_ref[0:3, g * 128 : g * 128 + 128] + p[0:3] * t[3:4] - t[0:3]
        for a in range(3):
            out_ref[a, g : g + 1, :] = force[a : a + 1]


def on_device(seg_data, cell_of_block, cell_center, pairs, live_count):
    nblocks, _, width = seg_data.shape
    ncell = cell_center.shape[1]
    slots = pairs.shape[0]
    vmem = pl.BlockSpec(memory_space=pltpu.VMEM)
    hbm = pl.BlockSpec(memory_space=pltpu.HBM)
    dma = pltpu.SemaphoreType.DMA
    far, window = pl.pallas_call(
        exchange_and_far,
        out_shape=(
            jax.ShapeDtypeStruct((3, nblocks * width), f32),
            jax.ShapeDtypeStruct((3, 8, ROWS, width), f32),
        ),
        in_specs=[hbm] * 5,
        out_specs=(vmem, vmem),
        scratch_shapes=[
            pltpu.VMEM((9, nblocks, width), f32),
            pltpu.VMEM((1, nblocks), jnp.int32),
            pltpu.VMEM((3, ncell), f32),
            pltpu.VMEM((2, slots), jnp.int32),
            pltpu.VMEM((1, 1), jnp.int32),
            pltpu.VMEM((nblocks, width), jnp.int32),
            pltpu.VMEM((ROWS, width), f32),
            pltpu.VMEM((16, nblocks * width), f32),
            pltpu.VMEM((16, ncell // 16), f32),
            pltpu.VMEM((7, 16, ncell // 16), f32),
            pltpu.VMEM((16, 16, ncell // 16), f32),
            pltpu.VMEM((ncell, 32), bf16),
            pltpu.VMEM((32, nblocks * width), bf16),
            pltpu.VMEM((32, nblocks * width), f32),
            dma((5,)), dma((2,)), dma((3, 4)), dma((3, 3)), dma((3, 8)),
            dma((7,)), dma((7,)), dma((16,)), dma((16,)), dma,
        ],
        compiler_params=pltpu.CompilerParams(
            collective_id=0, has_side_effects=True, vmem_limit_bytes=28 << 20
        ),
    )(
        seg_data.transpose(1, 0, 2), cell_of_block[None, :], cell_center, pairs.T,
        live_count[None, :],
    )
    force = pl.pallas_call(
        near_kernel,
        out_shape=jax.ShapeDtypeStruct((3, nblocks, width), f32),
        in_specs=[vmem, vmem],
        out_specs=vmem,
        scratch_shapes=[
            pltpu.VMEM((nblocks * width, 384), bf16),
            pltpu.VMEM((64, 384), bf16),
            pltpu.VMEM((nblocks, 16, width), f32),
            pltpu.VMEM((25 * 32, width), f32),
            pltpu.VMEM((8, width), jnp.int32),
            pltpu.SMEM((26 * 8, width), jnp.int32),
            pltpu.SemaphoreType.DMA,
        ],
        compiler_params=pltpu.CompilerParams(vmem_limit_bytes=28 << 20),
    )(window.reshape(24 * ROWS, width), far)
    return force.transpose(1, 0, 2)


def solution(mesh):
    placed = (
        P(("space", "sub"), None, None),
        P(("space", "sub")),
        P(),
        P(("space", "sub"), None),
        P(("space", "sub")),
    )
    return jax.shard_map(
        on_device,
        mesh=mesh,
        in_specs=placed,
        out_specs=P(("space", "sub"), None, None),
        check_vma=False,
    )
```

time: 86.7 us -> 60.6 us (0.70)
  the two profiles are of different devices: /device:TPU:33 before, /device:TPU:15 now
where the time goes in v2:
time: 60.6 us; the launch traced here: 60.4 us
  Pallas kernels  56.7 us (94%)
  local copies, waits for them, and re-layouts  3.08 us (5%)
  between operations  0.67 us (1%)
    pallas_call x1, Pallas kernels, on_device(): pl.pallas_call(exchange_and_far, out_shape=(jax.ShapeDtypeStruct((3, nblo...  40.5 us
    pallas_call x1, Pallas kernels, on_device(): pl.pallas_call(near_kernel, out_shape=jax.ShapeDtypeStruct((3, nblocks, w...  16.2 us
    unnamed x8, local copies, waits for them, and re-layouts  3.08 us

profile of v2, /device:TPU:15, one launch (start us, length us, event | category | flops | bytes accessed | tf_op | source)
XLA Modules:
  0.0 60.4 jit_solution(1690660169615147906)
XLA Ops:
  0.7 0.0 copy-start
  0.7 0.9 %copy-done = f32[32,9,128]{2,0,1:T(8,128)S(1)} copy-done((f32[32,9,128]{2,0,1:T(8,128)S(1)}, f32[32,9,128]{2,0,1:T(8,128)}, u32[]{:S(2)}) %copy-start) | copy-done | bytes 147480
  1.6 0.0 copy-start.1
  1.6 0.8 %copy-done.1 = f32[3,4096]{1,0:T(4,128)S(1)} copy-done((f32[3,4096]{1,0:T(4,128)S(1)}, f32[3,4096]{1,0:T(4,128)}, u32[]{:S(2)}) %copy-start.1) | copy-done | bytes 49176
  2.4 0.0 copy-start.2
  2.4 0.7 %copy-done.2 = s32[128,2]{0,1:T(2,128)S(1)} copy-done((s32[128,2]{0,1:T(2,128)S(1)}, s32[128,2]{0,1:T(2,128)}, u32[]{:S(2)}) %copy-start.2) | copy-done | bytes 1048
  3.1 0.0 copy-start.3
  3.1 0.7 %copy-done.3 = s32[32]{0:T(128)S(1)} copy-done((s32[32]{0:T(128)S(1)}, s32[32]{0:T(128)}, u32[]{:S(2)}) %copy-start.3) | copy-done | bytes 152
  3.7 40.5 %shard_map.55 = (f32[3,4096]{1,0:T(4,128)S(1)}, f32[3,8,296,128]{3,2,1,0:T(8,128)S(1)}) custom-call(f32[9,32,128]{2,1,0:T(8,128)S(1)} %bitcast.8, s32[1,32]{1,0:T(1,128)S(1)} %bitcast.10, f32[3,4096]{1,0:T(4,128)S(1)} %copy-done.1, s32[2,128]{1,0:T(2,128)S(1)} %bitcast.9, s32[1,1]{1,0:T(1,128)} %bitcast.6.live_hbm), custom_call_target="tpu_custom_call" | custom-call | tf_op jit(solution)/shard_map/pallas_call | solution.py:483
  44.2 16.2 %shard_map.56 = f32[3,32,128]{2,1,0:T(8,128)} custom-call(f32[7104,128]{1,0:T(8,128)S(1)} %bitcast.7, f32[3,4096]{1,0:T(4,128)S(1)} %get-tuple-element.8.far_ref), custom_call_target="tpu_custom_call" | custom-call | tf_op jit(solution)/shard_map/pallas_call | solution.py:516
Async XLA Ops:
  0.7 0.9 %copy-start = (f32[32,9,128]{2,0,1:T(8,128)S(1)}, f32[32,9,128]{2,0,1:T(8,128)}, u32[]{:S(2)}) copy-start(f32[32,9,128]{2,0,1:T(8,128)} %param.5) | copy-start | bytes 442372
  1.6 0.8 %copy-start.1 = (f32[3,4096]{1,0:T(4,128)S(1)}, f32[3,4096]{1,0:T(4,128)}, u32[]{:S(2)}) copy-start(f32[3,4096]{1,0:T(4,128)} %cc_hbm.1) | copy-start | bytes 147460
  2.4 0.7 %copy-start.2 = (s32[128,2]{0,1:T(2,128)S(1)}, s32[128,2]{0,1:T(2,128)}, u32[]{:S(2)}) copy-start(s32[128,2]{0,1:T(2,128)} %param.8) | copy-start | bytes 3076
  3.1 0.7 %copy-start.3 = (s32[32]{0:T(128)S(1)}, s32[32]{0:T(128)}, u32[]{:S(2)}) copy-start(s32[32]{0:T(128)} %param.6) | copy-start | bytes 388

commit v3 on v2

--- a/solution.py
+++ b/solution.py
@@ -12,7 +12,7 @@
 bf16 = jnp.bfloat16
 ROWS = 296
 UNROLL = 8
-SEG_TILE = 2048
+EARLY = 3
 
 
 def three(x):
@@ -23,10 +23,10 @@
 
 
 def exchange_and_far(
-    seg_hbm, cell_hbm, cc_hbm, pair_hbm, live_hbm, far_ref, win_ref,
+    seg_hbm, cell_hbm, cc_hbm, pair_hbm, live_hbm, far_hbm, win_ref,
     seg_ref, cell_row, cc_ref, pair_ref, live_ref, cell_ref,
-    payload, flat, mine, parts, moments, cells_f, segs_f, acc,
-    in_sem, x_send, w_send, r_send, w_recv, p_send, p_recv, m_send, m_recv, own_sem,
+    payload, flat, mine, parts, moments, cells_f, segs_f, acc, early, far_ref,
+    in_sem, x_send, w_send, r_send, w_recv, p_send, p_recv, m_send, m_recv, own_sem, far_sem,
 ):
     space = lax.axis_index("space")
     sub = lax.axis_index("sub")
@@ -149,7 +149,16 @@
             device_id=(space, z * 2 + 1 - core), device_id_type=MESH,
         )
 
-    for k in (1, 3, 2, 0):
+    def forward(slot):
+        step = 1 + 2 * core
+        place = (z + 4 - step) % 4 * 2 + core
+        return pltpu.make_async_remote_copy(
+            src_ref=win_ref.at[slot, place], dst_ref=win_ref.at[slot, place],
+            send_sem=w_send.at[slot, 2], recv_sem=w_recv.at[slot, place],
+            device_id=(space, (z + step) % 4 * 2 + core), device_id_type=MESH,
+        )
+
+    for k in (1, 3, 0):
         spread(1, k).start()
 
     for g in range(nblocks):
@@ -173,6 +182,37 @@
         [p1, p2, p1, p2, p3, p1, ones, pq, blank], axis=0
     ).astype(bf16)
 
+    def split_moments(k):
+        m = moments[k]
+        hi = m.astype(bf16)
+        return jnp.concatenate([hi, (m - hi.astype(f32)).astype(bf16)], axis=0)
+
+    def weights(k, first):
+        at = pl.multiple_of((space + k) % 16 * per, 256)
+        dist = jnp.dot(cells_f[pl.ds(at, per), :], segs_f[...], preferred_element_type=f32)
+        w = pl.reciprocal(dist, approx=True)
+        if first:
+            cell_id = at + lax.broadcasted_iota(jnp.int32, (per, 128), 0)
+            w = jnp.concatenate(
+                [
+                    jnp.where(
+                        cell_id == cell_ref[g : g + 1, :], 0.0, w[:, g * 128 : g * 128 + 128]
+                    )
+                    for g in range(nblocks)
+                ],
+                axis=1,
+            )
+        hi = w.astype(bf16)
+        return hi, (w - hi.astype(f32)).astype(bf16)
+
+    def product(k, hi, lo):
+        m = split_moments(k)
+        return jnp.dot(m, hi, preferred_element_type=f32) + jnp.dot(
+            m, lo, preferred_element_type=f32
+        )
+
+    early[0, 0], early[0, 1] = weights(0, True)
+
     region = mine[...]
     for k in range(7):
         pltpu.make_async_copy(parts.at[k], parts.at[k], p_recv.at[k]).wait()
@@ -192,63 +232,46 @@
 
     lax.fori_loop(1, 16, start_moment, 0)
 
-    def split_moments(k):
-        m = moments[k]
-        hi = m.astype(bf16)
-        return jnp.concatenate([hi, (m - hi.astype(f32)).astype(bf16)], axis=0)
-
-    def far_chunk(k, first):
-        at = pl.multiple_of((space + k) % 16 * per, 256)
-        cells = cells_f[pl.ds(at, per), :]
-        m = split_moments(k)
-        cell_id = at + lax.broadcasted_iota(jnp.int32, (per, 128), 0)
-
-        def tile(j, carry):
-            lanes = pl.ds(pl.multiple_of(j * SEG_TILE, SEG_TILE), SEG_TILE)
-            d = jnp.dot(cells, segs_f[:, lanes], preferred_element_type=f32)
-            w = pl.reciprocal(d, approx=True)
-            if first:
-                cols = []
-                for q in range(SEG_TILE // 128):
-                    block = cell_ref[pl.ds(j * (SEG_TILE // 128) + q, 1), :]
-                    cols.append(
-                        jnp.where(cell_id == block, 0.0, w[:, q * 128 : q * 128 + 128])
-                    )
-                w = jnp.concatenate(cols, axis=1)
-            hi = w.astype(bf16)
-            lo = (w - hi.astype(f32)).astype(bf16)
-            g = jnp.dot(m, hi, preferred_element_type=f32)
-            g = g + jnp.dot(m, lo, preferred_element_type=f32)
-            if first:
-                acc[:, lanes] = g
-            else:
-                acc[:, lanes] += g
-            return carry
-
-        lax.fori_loop(0, nblocks * 128 // SEG_TILE, tile, 0)
+    for k in range(1, EARLY):
+        early[k, 0], early[k, 1] = weights(k, False)
+    acc[...] = product(0, early[0, 0], early[0, 1])
+
+    def moments_here(k):
+        pltpu.make_async_copy(moments.at[k], moments.at[k], m_recv.at[k]).wait()
 
     def later_chunk(k, carry):
-        pltpu.make_async_copy(moments.at[k], moments.at[k], m_recv.at[k]).wait()
-        far_chunk(k, False)
+        moments_here(k)
+        hi, lo = weights(k, False)
+        acc[...] += product(k, hi, lo)
         return carry
 
-    far_chunk(0, True)
-    lax.fori_loop(1, 3, later_chunk, 0)
-    arrived(0, sub)
-    arrived(2, sub)
+    def chip(k):
+        return (z + k) % 4 * 2 + core
+
     for slot in (0, 2):
-        for k in (1, 3, 2, 0):
+        arrived(slot, sub)
+        for k in (1, 3, 0):
             spread(slot, k).start()
-    lax.fori_loop(3, 6, later_chunk, 0)
-    for k in (1, 3, 2):
-        arrived(1, (z + k) % 4 * 2 + core)
+    for k in range(1, EARLY):
+        moments_here(k)
+        acc[...] += product(k, early[k, 0], early[k, 1])
+    for k in (1, 3):
+        arrived(1, chip(k))
+    forward(1).start()
+    for k in (1, 3):
         relay(1, k).start()
-    lax.fori_loop(6, 13, later_chunk, 0)
+    lax.fori_loop(EARLY, 8, later_chunk, 0)
     for slot in (0, 2):
-        for k in (1, 3, 2):
-            arrived(slot, (z + k) % 4 * 2 + core)
+        for k in (1, 3):
+            arrived(slot, chip(k))
+        forward(slot).start()
+        for k in (1, 3):
             relay(slot, k).start()
-    lax.fori_loop(13, 16, later_chunk, 0)
+    lax.fori_loop(8, 11, later_chunk, 0)
+    for slot in range(3):
+        arrived(slot, chip(2))
+        relay(slot, 2).start()
+    lax.fori_loop(11, 16, later_chunk, 0)
 
     grid = acc[0:9, :] + acc[16:25, :]
     line = flat[8:11, :]
@@ -257,16 +280,21 @@
             grid[3 * a : 3 * a + 3, :] * line, axis=0, keepdims=True
         )
 
+    far_copy = pltpu.make_async_copy(far_ref, far_hbm, far_sem)
+    far_copy.start()
+
     other = 1 - core
     for slot in range(3):
         for k in range(4):
             arrived(slot, (z + k) % 4 * 2 + other)
     own_copy.wait()
+    far_copy.wait()
     right.wait_send()
     left.wait_send()
     for slot in range(3):
-        for k in range(4):
+        for k in (0, 1, 3):
             spread(slot, k).wait_send()
+        forward(slot).wait_send()
         for k in range(1, 4):
             relay(slot, k).wait_send()
 
@@ -311,16 +339,15 @@
     return a.astype(bf16), b.astype(bf16), c.astype(bf16), ext.astype(bf16)
 
 
-def build_list(win_ref, space, sub, nblocks, hots, listed, table, sem):
-    my_row = (8 + sub) * ROWS
+def build_list(pair_ref, space, sub, nblocks, hots, listed, table, sem):
     first_block = ((space * 8 + sub) * nblocks).astype(f32)
     target = jnp.concatenate(
-        [win_ref[d * ROWS + 288 : d * ROWS + 289, :] for d in range(24)]
-        + [win_ref[pl.ds(my_row + 288, 1), :]], axis=0
+        [pair_ref[d, 0:1, :] for d in range(24)] + [pair_ref[8 + sub, 0:1, :]],
+        axis=0,
     )
     source = jnp.concatenate(
-        [win_ref[d * ROWS + 289 : d * ROWS + 290, :] for d in range(24)]
-        + [win_ref[pl.ds(my_row + 289, 1), :]], axis=0
+        [pair_ref[d, 1:2, :] for d in range(24)] + [pair_ref[8 + sub, 1:2, :]],
+        axis=0,
     )
     is_own = lax.broadcasted_iota(jnp.int32, (25, 128), 0) == 24
     mine = jnp.where(is_own, target, source) - first_block
@@ -395,14 +422,25 @@
     return count
 
 
-def near_kernel(win_ref, far_ref, out_ref, feats, arrange, acc, hots, listed, table, sem):
+def near_kernel(
+    win_hbm, pair_hbm, far_hbm, out_ref,
+    win_ref, pair_ref, own_ref, far_ref, feats, arrange, acc, hots, listed, table, sem, in_sem,
+):
     space, sub = lax.axis_index("space"), lax.axis_index("sub")
     nblocks = out_ref.shape[1]
-    my_row = (8 + sub) * ROWS
+    my_row = pl.multiple_of((8 + sub) * ROWS, 8)
+    pairs_in = pltpu.make_async_copy(pair_hbm.at[:, 288:296], pair_ref, in_sem.at[0])
+    own_in = pltpu.make_async_copy(win_hbm.at[pl.ds(my_row, ROWS)], own_ref, in_sem.at[1])
+    win_in = pltpu.make_async_copy(win_hbm, win_ref, in_sem.at[2])
+    far_in = pltpu.make_async_copy(far_hbm, far_ref, in_sem.at[3])
+    for copy in (pairs_in, own_in, win_in, far_in):
+        copy.start()
+    pairs_in.wait()
+    count = build_list(pair_ref, space, sub, nblocks, hots, listed, table, sem)
+    own_in.wait()
     origin = jnp.where(
-        lax.broadcasted_iota(jnp.int32, (16, 1), 0) < 3, win_ref[pl.ds(my_row, 16), 0:1], 0.0
-    )
-    count = build_list(win_ref, space, sub, nblocks, hots, listed, table, sem)
+        lax.broadcasted_iota(jnp.int32, (16, 1), 0) < 3, own_ref[0:16, 0:1], 0.0
+    )
 
     arrange[...] = arrangement()
     acc[...] = jnp.zeros_like(acc)
@@ -410,7 +448,7 @@
         x = jnp.concatenate(
             [
                 jnp.concatenate(
-                    split_rows(win_ref[pl.ds(my_row + 9 * g, 16), :] - origin, 0.25), axis=0
+                    split_rows(own_ref[9 * g : 9 * g + 16, :] - origin, 0.25), axis=0
                 )
                 for g in range(q, q + 8)
             ],
@@ -421,6 +459,7 @@
         )
         feats[q * 128 : q * 128 + 1024, :] = f.astype(bf16)
 
+    win_in.wait()
     half = lax.broadcasted_iota(jnp.int32, (1, 256), 1) < 128
     top = lax.broadcasted_iota(jnp.int32, (16, 128), 0) < 3
 
@@ -465,8 +504,9 @@
 
     lax.fori_loop(0, (count // 2 + UNROLL - 1) // UNROLL, items, 0)
 
+    far_in.wait()
     for g in range(nblocks):
-        p = win_ref[pl.ds(my_row + 9 * g, 16), :] - origin
+        p = own_ref[9 * g : 9 * g + 16, :] - origin
         t = acc[g]
         force = far_ref[0:3, g * 128 : g * 128 + 128] + p[0:3] * t[3:4] - t[0:3]
         for a in range(3):
@@ -487,7 +527,7 @@
             jax.ShapeDtypeStruct((3, 8, ROWS, width), f32),
         ),
         in_specs=[hbm] * 5,
-        out_specs=(vmem, vmem),
+        out_specs=(hbm, hbm),
         scratch_shapes=[
             pltpu.VMEM((9, nblocks, width), f32),
             pltpu.VMEM((1, nblocks), jnp.int32),
@@ -503,11 +543,13 @@
             pltpu.VMEM((ncell, 32), bf16),
             pltpu.VMEM((32, nblocks * width), bf16),
             pltpu.VMEM((32, nblocks * width), f32),
+            pltpu.VMEM((EARLY, 2, ncell // 16, nblocks * width), bf16),
+            pltpu.VMEM((3, nblocks * width), f32),
             dma((5,)), dma((2,)), dma((3, 4)), dma((3, 3)), dma((3, 8)),
-            dma((7,)), dma((7,)), dma((16,)), dma((16,)), dma,
+            dma((7,)), dma((7,)), dma((16,)), dma((16,)), dma, dma,
         ],
         compiler_params=pltpu.CompilerParams(
-            collective_id=0, has_side_effects=True, vmem_limit_bytes=28 << 20
+            collective_id=0, has_side_effects=True, vmem_limit_bytes=56 << 20
         ),
     )(
         seg_data.transpose(1, 0, 2), cell_of_block[None, :], cell_center, pairs.T,
@@ -516,19 +558,23 @@
     force = pl.pallas_call(
         near_kernel,
         out_shape=jax.ShapeDtypeStruct((3, nblocks, width), f32),
-        in_specs=[vmem, vmem],
+        in_specs=[hbm] * 3,
         out_specs=vmem,
         scratch_shapes=[
+            pltpu.VMEM((24 * ROWS, width), f32),
+            pltpu.VMEM((24, 8, width), f32),
+            pltpu.VMEM((ROWS, width), f32),
+            pltpu.VMEM((3, nblocks * width), f32),
             pltpu.VMEM((nblocks * width, 384), bf16),
             pltpu.VMEM((64, 384), bf16),
             pltpu.VMEM((nblocks, 16, width), f32),
             pltpu.VMEM((25 * 32, width), f32),
             pltpu.VMEM((8, width), jnp.int32),
             pltpu.SMEM((26 * 8, width), jnp.int32),
-            pltpu.SemaphoreType.DMA,
+            dma, dma((4,)),
         ],
-        compiler_params=pltpu.CompilerParams(vmem_limit_bytes=28 << 20),
-    )(window.reshape(24 * ROWS, width), far)
+        compiler_params=pltpu.CompilerParams(vmem_limit_bytes=56 << 20),
+    )(window.reshape(24 * ROWS, width), window.reshape(24, ROWS, width), far)
     return force.transpose(1, 0, 2)
 
 

time: 60.6 us -> 58.6 us (0.967)
  the two profiles are of different devices: /device:TPU:15 before, /device:TPU:32 now
where the time goes in v3:
time: 58.6 us; the launch traced here: 58.5 us
  Pallas kernels  57.8 us (99%)
  between operations  0.66 us (1%)
    pallas_call x1, Pallas kernels, on_device(): pl.pallas_call(exchange_and_far, out_shape=(jax.ShapeDtypeStruct((3, nblo...  39.7 us
    pallas_call x1, Pallas kernels, on_device(): pl.pallas_call(near_kernel, out_shape=jax.ShapeDtypeStruct((3, nblocks, w...  18.1 us

profile of v3, /device:TPU:32, one launch (start us, length us, event | category | flops | bytes accessed | tf_op | source)
XLA Modules:
  0.0 58.5 jit_solution(6107714702338508605)
XLA Ops:
  0.7 39.7 %shard_map.55 = (f32[3,4096]{1,0:T(4,128)}, f32[3,8,296,128]{3,2,1,0:T(8,128)}) custom-call(f32[9,32,128]{2,1,0:T(8,128)} %bitcast.10, s32[1,32]{1,0:T(1,128)} %bitcast.12, f32[3,4096]{1,0:T(4,128)} %cc_hbm.1, s32[2,128]{1,0:T(2,128)} %bitcast.11, s32[1,1]{1,0:T(1,128)} %bitcast.7.live_hbm), custom_call_target="tpu_custom_call" | custom-call | tf_op jit(solution)/shard_map/pallas_call | solution.py:523
  40.3 18.1 %shard_map.56 = f32[3,32,128]{2,1,0:T(8,128)} custom-call(f32[7104,128]{1,0:T(8,128)} %bitcast.8, f32[24,296,128]{2,1,0:T(8,128)} %bitcast.9, f32[3,4096]{1,0:T(4,128)} %get-tuple-element.8.far_hbm), custom_call_target="tpu_custom_call" | custom-call | tf_op jit(solution)/shard_map/pallas_call | solution.py:558

commit v4 on v3

--- a/solution.py
+++ b/solution.py
@@ -12,7 +12,6 @@
 bf16 = jnp.bfloat16
 ROWS = 296
 UNROLL = 8
-EARLY = 3
 
 
 def three(x):
@@ -23,17 +22,32 @@
 
 
 def exchange_and_far(
-    seg_hbm, cell_hbm, cc_hbm, pair_hbm, live_hbm, far_hbm, win_ref,
+    seg_hbm, cell_hbm, cc_hbm, pair_hbm, live_hbm, far_hbm, win,
     seg_ref, cell_row, cc_ref, pair_ref, live_ref, cell_ref,
-    payload, flat, mine, parts, moments, cells_f, segs_f, acc, early, far_ref,
-    in_sem, x_send, w_send, r_send, w_recv, p_send, p_recv, m_send, m_recv, own_sem, far_sem,
+    payload, flat, mine, twin, pair_sum, parts, moments, cells_f, segs_f, acc, early, far_ref,
+    in_sem, x_send, x_recv, z_send, z_recv, r_send, r_recv,
+    twin_send, twin_recv, p_send, p_recv, y_send, y_recv, m_send, m_recv, own_sem, far_sem,
 ):
     space = lax.axis_index("space")
     sub = lax.axis_index("sub")
+    y, x = space // 4, space % 4
     z, core = sub // 2, sub % 2
     nblocks = seg_ref.shape[1]
     ncell = cc_ref.shape[1]
     per = ncell // 16
+    other_core = (space, z * 2 + 1 - core)
+
+    def along_z(k):
+        return (space, (z + k) % 4 * 2 + core)
+
+    def along_y(k):
+        return ((y + k) % 4 * 4 + x, sub)
+
+    def along_x(k):
+        return (y * 4 + (x + k) % 4, sub)
+
+    def along_space(k):
+        return ((space + k) % 16, sub)
 
     ins = [
         pltpu.make_async_copy(src, dst, in_sem.at[i])
@@ -47,21 +61,10 @@
     for copy in ins:
         copy.start()
     barrier = pltpu.get_barrier_semaphore()
-
-    def greet_sub(k, c):
-        pl.semaphore_signal(
-            barrier, inc=1, device_id=(space, (sub + k) % 8), device_id_type=MESH
-        )
-        return c
-
-    def greet_space(k, c):
-        pl.semaphore_signal(
-            barrier, inc=1, device_id=((space + k) % 16, sub), device_id_type=MESH
-        )
-        return c
-
-    lax.fori_loop(1, 8, greet_sub, 0)
-    lax.fori_loop(1, 16, greet_space, 0)
+    partners = [other_core, along_space(1), along_space(15)]
+    partners += [to(k) for to in (along_z, along_y, along_x) for k in (1, 2, 3)]
+    for to in partners:
+        pl.semaphore_signal(barrier, inc=1, device_id=to, device_id_type=MESH)
 
     for copy in ins:
         copy.wait()
@@ -91,75 +94,64 @@
     for a in range(3):
         for b in range(3):
             outer = jnp.sum(seg_ref[6 + a] * seg_ref[3 + b], axis=1, keepdims=True)
-            mine[3 * a + b : 3 * a + b + 1, :] = jnp.sum(hot * outer, axis=0, keepdims=True)
-    mine[9:16, :] = jnp.zeros((7, per), f32)
-
-    pl.semaphore_wait(barrier, 22)
-
-    def part_copy(k):
-        to = (sub + k) % 8
+            row = jnp.sum(hot * outer, axis=0, keepdims=True)
+            mine[3 * a + b : 3 * a + b + 1, :] = row[:, 0:128]
+            mine[9 + 3 * a + b : 10 + 3 * a + b, :] = row[:, 128:256]
+
+    def send(src, dst, send_sem, recv_sem, to):
         return pltpu.make_async_remote_copy(
-            src_ref=mine, dst_ref=parts.at[7 - k],
-            send_sem=p_send.at[k - 1], recv_sem=p_recv.at[7 - k],
-            device_id=(space, to), device_id_type=MESH,
-        )
-
-
-    def start_part(k, c):
-        part_copy(k).start()
-        return c
-
-    lax.fori_loop(1, 8, start_part, 0)
-
-    def beside(step, slot, sem):
-        return pltpu.make_async_remote_copy(
-            src_ref=payload, dst_ref=win_ref.at[slot, sub],
-            send_sem=x_send.at[sem], recv_sem=w_recv.at[slot, sub],
-            device_id=((space + step) % 16, sub), device_id_type=MESH,
-        )
-
-    right, left = beside(1, 0, 0), beside(15, 2, 1)
-    right.start()
-    left.start()
-    own_copy = pltpu.make_async_copy(payload, win_ref.at[1, sub], own_sem)
+            src_ref=src, dst_ref=dst, send_sem=send_sem, recv_sem=recv_sem,
+            device_id=to, device_id_type=MESH,
+        )
+
+    def arrived(ref, sem):
+        pltpu.make_async_copy(ref, ref, sem).wait()
+
+    own_copy = pltpu.make_async_copy(payload, win.at[core, 0], own_sem)
     own_copy.start()
-
-    def spread(slot, k):
-        src = payload if slot == 1 else win_ref.at[slot, sub]
-        if k == 0:
-            to = z * 2 + 1 - core
-        else:
-            to = (z + k) % 4 * 2 + core
-        return pltpu.make_async_remote_copy(
-            src_ref=src, dst_ref=win_ref.at[slot, sub],
-            send_sem=w_send.at[slot, k], recv_sem=w_recv.at[slot, sub],
-            device_id=(space, to), device_id_type=MESH,
-        )
-
-    def arrived(slot, place):
-        pltpu.make_async_copy(
-            win_ref.at[slot, place], win_ref.at[slot, place], w_recv.at[slot, place]
-        ).wait()
-
-    def relay(slot, k):
-        place = (z + k) % 4 * 2 + core
-        return pltpu.make_async_remote_copy(
-            src_ref=win_ref.at[slot, place], dst_ref=win_ref.at[slot, place],
-            send_sem=r_send.at[slot, k - 1], recv_sem=w_recv.at[slot, place],
-            device_id=(space, z * 2 + 1 - core), device_id_type=MESH,
-        )
-
-    def forward(slot):
-        step = 1 + 2 * core
-        place = (z + 4 - step) % 4 * 2 + core
-        return pltpu.make_async_remote_copy(
-            src_ref=win_ref.at[slot, place], dst_ref=win_ref.at[slot, place],
-            send_sem=w_send.at[slot, 2], recv_sem=w_recv.at[slot, place],
-            device_id=(space, (z + step) % 4 * 2 + core), device_id_type=MESH,
-        )
-
-    for k in (1, 3, 0):
-        spread(1, k).start()
+    pl.semaphore_wait(barrier, len(partners))
+
+    to_twin = send(mine, twin, twin_send, twin_recv, other_core)
+    to_z = [
+        send(pair_sum, parts.at[3 - k], p_send.at[k - 1], p_recv.at[3 - k], along_z(k))
+        for k in (1, 2, 3)
+    ]
+    to_y = [
+        send(moments.at[0, 0], moments.at[0, 4 - k], y_send.at[k - 1], y_recv.at[3 - k], along_y(k))
+        for k in (1, 2, 3)
+    ]
+    to_x = [
+        send(moments.at[0], moments.at[4 - k], m_send.at[k - 1], m_recv.at[3 - k], along_x(k))
+        for k in (1, 2, 3)
+    ]
+    after = send(payload, win.at[core, 4], x_send.at[0], x_recv.at[0], along_space(1))
+    before = send(payload, win.at[core, 5], x_send.at[1], x_recv.at[1], along_space(15))
+    step = 1 + 2 * core
+
+    def place(group, dz):
+        return win.at[core, dz] if group == 0 else win.at[core, pl.ds(4 + 2 * dz, 2)]
+
+    def spread(group, k):
+        return send(
+            payload if group == 0 else place(1, 0), place(group, 4 - k),
+            z_send.at[group, k // 2], z_recv.at[group, 3 - k], along_z(k),
+        )
+
+    def forward(group):
+        return send(
+            place(group, 4 - step), place(group, 2),
+            z_send.at[group, 2], z_recv.at[group, 1], along_z(step),
+        )
+
+    def relay(group):
+        part = win.at[core, 0:4] if group == 0 else win.at[core, 4:12]
+        return send(part, part, r_send.at[group], r_recv.at[group], other_core)
+
+    to_twin.start()
+    after.start()
+    before.start()
+    for k in (1, 3):
+        spread(0, k).start()
 
     for g in range(nblocks):
         lanes = slice(g * 128, g * 128 + 128)
@@ -182,13 +174,11 @@
         [p1, p2, p1, p2, p3, p1, ones, pq, blank], axis=0
     ).astype(bf16)
 
-    def split_moments(k):
-        m = moments[k]
-        hi = m.astype(bf16)
-        return jnp.concatenate([hi, (m - hi.astype(f32)).astype(bf16)], axis=0)
-
-    def weights(k, first):
-        at = pl.multiple_of((space + k) % 16 * per, 256)
+    def region_of(dx, dy):
+        return (y + dy) % 4 * 4 + (x + dx) % 4
+
+    def weights(region, first):
+        at = pl.multiple_of(region * per, 256)
         dist = jnp.dot(cells_f[pl.ds(at, per), :], segs_f[...], preferred_element_type=f32)
         w = pl.reciprocal(dist, approx=True)
         if first:
@@ -205,73 +195,72 @@
         hi = w.astype(bf16)
         return hi, (w - hi.astype(f32)).astype(bf16)
 
-    def product(k, hi, lo):
-        m = split_moments(k)
+    def product(dx, dy, hi, lo):
+        m = moments[dx, dy]
+        m = jnp.concatenate([m[0:9], m[9:18]], axis=1)
+        m = jnp.concatenate([m, jnp.zeros((7, per), f32)], axis=0)
+        m_hi = m.astype(bf16)
+        m = jnp.concatenate([m_hi, (m - m_hi.astype(f32)).astype(bf16)], axis=0)
         return jnp.dot(m, hi, preferred_element_type=f32) + jnp.dot(
             m, lo, preferred_element_type=f32
         )
 
-    early[0, 0], early[0, 1] = weights(0, True)
-
-    region = mine[...]
-    for k in range(7):
-        pltpu.make_async_copy(parts.at[k], parts.at[k], p_recv.at[k]).wait()
+    early[0, 0], early[0, 1] = weights(space, True)
+
+    arrived(twin, twin_recv)
+    pair_sum[...] = mine[...] + twin[...]
+    for copy in to_z:
+        copy.start()
+    early[1, 0], early[1, 1] = weights(region_of(0, 1), False)
+
+    region = pair_sum[...]
+    for k in range(3):
+        arrived(parts.at[k], p_recv.at[k])
         region = region + parts[k]
-    moments[0] = region
-
-    def moment_copy(k):
-        return pltpu.make_async_remote_copy(
-            src_ref=moments.at[0], dst_ref=moments.at[16 - k],
-            send_sem=m_send.at[k], recv_sem=m_recv.at[16 - k],
-            device_id=((space + k) % 16, sub), device_id_type=MESH,
-        )
-
-    def start_moment(k, c):
-        moment_copy(k).start()
-        return c
-
-    lax.fori_loop(1, 16, start_moment, 0)
-
-    for k in range(1, EARLY):
-        early[k, 0], early[k, 1] = weights(k, False)
-    acc[...] = product(0, early[0, 0], early[0, 1])
-
-    def moments_here(k):
-        pltpu.make_async_copy(moments.at[k], moments.at[k], m_recv.at[k]).wait()
+    moments[0, 0] = region
+    for copy in to_y:
+        copy.start()
+    early[2, 0], early[2, 1] = weights(region_of(0, 2), False)
+
+    for k in range(3):
+        arrived(moments.at[0, k + 1], y_recv.at[k])
+    for copy in to_x:
+        copy.start()
+    for k in range(2):
+        arrived(win.at[core, 4 + k], x_recv.at[k])
+    for k in (1, 3):
+        spread(1, k).start()
+    early[3, 0], early[3, 1] = weights(region_of(0, 3), False)
+
+    for dz in (1, 3):
+        arrived(place(0, dz), z_recv.at[0, dz - 1])
+    forward(0).start()
+    acc[...] = product(0, 0, early[0, 0], early[0, 1])
+    for k in range(1, 4):
+        acc[...] += product(0, k, early[k, 0], early[k, 1])
 
     def later_chunk(k, carry):
-        moments_here(k)
-        hi, lo = weights(k, False)
-        acc[...] += product(k, hi, lo)
+        dx, dy = k // 4, k % 4
+        hi, lo = weights(region_of(dx, dy), False)
+        acc[...] += product(dx, dy, hi, lo)
         return carry
 
-    def chip(k):
-        return (z + k) % 4 * 2 + core
-
-    for slot in (0, 2):
-        arrived(slot, sub)
-        for k in (1, 3, 0):
-            spread(slot, k).start()
-    for k in range(1, EARLY):
-        moments_here(k)
-        acc[...] += product(k, early[k, 0], early[k, 1])
-    for k in (1, 3):
-        arrived(1, chip(k))
+    arrived(moments.at[1], m_recv.at[0])
+    lax.fori_loop(4, 6, later_chunk, 0)
+    arrived(place(0, 2), z_recv.at[0, 1])
+    own_copy.wait()
+    relay(0).start()
+    lax.fori_loop(6, 8, later_chunk, 0)
+    arrived(moments.at[2], m_recv.at[1])
+    lax.fori_loop(8, 9, later_chunk, 0)
+    for dz in (1, 3):
+        arrived(place(1, dz), z_recv.at[1, dz - 1])
     forward(1).start()
-    for k in (1, 3):
-        relay(1, k).start()
-    lax.fori_loop(EARLY, 8, later_chunk, 0)
-    for slot in (0, 2):
-        for k in (1, 3):
-            arrived(slot, chip(k))
-        forward(slot).start()
-        for k in (1, 3):
-            relay(slot, k).start()
-    lax.fori_loop(8, 11, later_chunk, 0)
-    for slot in range(3):
-        arrived(slot, chip(2))
-        relay(slot, 2).start()
-    lax.fori_loop(11, 16, later_chunk, 0)
+    lax.fori_loop(9, 12, later_chunk, 0)
+    arrived(place(1, 2), z_recv.at[1, 1])
+    relay(1).start()
+    arrived(moments.at[3], m_recv.at[2])
+    lax.fori_loop(12, 16, later_chunk, 0)
 
     grid = acc[0:9, :] + acc[16:25, :]
     line = flat[8:11, :]
@@ -283,31 +272,16 @@
     far_copy = pltpu.make_async_copy(far_ref, far_hbm, far_sem)
     far_copy.start()
 
-    other = 1 - core
-    for slot in range(3):
-        for k in range(4):
-            arrived(slot, (z + k) % 4 * 2 + other)
-    own_copy.wait()
+    arrived(win.at[1 - core, 0:4], r_recv.at[0])
+    arrived(win.at[1 - core, 4:12], r_recv.at[1])
+    for copy in [to_twin, after, before] + to_z + to_y + to_x:
+        copy.wait_send()
+    for group in range(2):
+        for k in (1, 3):
+            spread(group, k).wait_send()
+        forward(group).wait_send()
+        relay(group).wait_send()
     far_copy.wait()
-    right.wait_send()
-    left.wait_send()
-    for slot in range(3):
-        for k in (0, 1, 3):
-            spread(slot, k).wait_send()
-        forward(slot).wait_send()
-        for k in range(1, 4):
-            relay(slot, k).wait_send()
-
-    def end_part(k, c):
-        part_copy(k).wait_send()
-        return c
-
-    def end_moment(k, c):
-        moment_copy(k).wait_send()
-        return c
-
-    lax.fori_loop(1, 8, end_part, 0)
-    lax.fori_loop(1, 16, end_moment, 0)
 
 
 def arrangement():
@@ -342,11 +316,11 @@
 def build_list(pair_ref, space, sub, nblocks, hots, listed, table, sem):
     first_block = ((space * 8 + sub) * nblocks).astype(f32)
     target = jnp.concatenate(
-        [pair_ref[d, 0:1, :] for d in range(24)] + [pair_ref[8 + sub, 0:1, :]],
+        [pair_ref[d, 0:1, :] for d in range(24)] + [pair_ref[sub % 2 * 12, 0:1, :]],
         axis=0,
     )
     source = jnp.concatenate(
-        [pair_ref[d, 1:2, :] for d in range(24)] + [pair_ref[8 + sub, 1:2, :]],
+        [pair_ref[d, 1:2, :] for d in range(24)] + [pair_ref[sub % 2 * 12, 1:2, :]],
         axis=0,
     )
     is_own = lax.broadcasted_iota(jnp.int32, (25, 128), 0) == 24
@@ -356,9 +330,15 @@
     mine = jnp.where(used, mine, -1.0)
     owner = jnp.floor(theirs * (1.0 / 32))
     their_space = jnp.floor(owner * (1.0 / 8))
-    ahead = their_space - space.astype(f32) + 1.0
-    ahead = jnp.where(ahead < 0, ahead + 16.0, jnp.where(ahead >= 16, ahead - 16.0, ahead))
-    dev = ahead * 8.0 + (owner - 8.0 * their_space)
+    their_sub = owner - 8.0 * their_space
+    their_z = jnp.floor(their_sub * 0.5)
+    ahead = their_space - space.astype(f32)
+    ahead = jnp.where(ahead < -8, ahead + 16.0, jnp.where(ahead > 8, ahead - 16.0, ahead))
+    dz = their_z - (sub // 2).astype(f32)
+    dz = jnp.where(dz < 0, dz + 4.0, dz)
+    dev = (their_sub - 2.0 * their_z) * 12.0 + jnp.where(
+        ahead == 0, dz, 4.0 + 2.0 * dz + (ahead > 0).astype(f32)
+    )
     local = theirs - 32.0 * owner
     before = (
         lax.broadcasted_iota(jnp.int32, (128, 128), 0)
@@ -428,7 +408,7 @@
 ):
     space, sub = lax.axis_index("space"), lax.axis_index("sub")
     nblocks = out_ref.shape[1]
-    my_row = pl.multiple_of((8 + sub) * ROWS, 8)
+    my_row = pl.multiple_of(sub % 2 * 12 * ROWS, 8)
     pairs_in = pltpu.make_async_copy(pair_hbm.at[:, 288:296], pair_ref, in_sem.at[0])
     own_in = pltpu.make_async_copy(win_hbm.at[pl.ds(my_row, ROWS)], own_ref, in_sem.at[1])
     win_in = pltpu.make_async_copy(win_hbm, win_ref, in_sem.at[2])
@@ -524,7 +504,7 @@
         exchange_and_far,
         out_shape=(
             jax.ShapeDtypeStruct((3, nblocks * width), f32),
-            jax.ShapeDtypeStruct((3, 8, ROWS, width), f32),
+            jax.ShapeDtypeStruct((2, 12, ROWS, width), f32),
         ),
         in_specs=[hbm] * 5,
         out_specs=(hbm, hbm),
@@ -537,16 +517,18 @@
             pltpu.VMEM((nblocks, width), jnp.int32),
             pltpu.VMEM((ROWS, width), f32),
             pltpu.VMEM((16, nblocks * width), f32),
-            pltpu.VMEM((16, ncell // 16), f32),
-            pltpu.VMEM((7, 16, ncell // 16), f32),
-            pltpu.VMEM((16, 16, ncell // 16), f32),
+            pltpu.VMEM((18, 128), f32),
+            pltpu.VMEM((18, 128), f32),
+            pltpu.VMEM((18, 128), f32),
+            pltpu.VMEM((3, 18, 128), f32),
+            pltpu.VMEM((4, 4, 18, 128), f32),
             pltpu.VMEM((ncell, 32), bf16),
             pltpu.VMEM((32, nblocks * width), bf16),
             pltpu.VMEM((32, nblocks * width), f32),
-            pltpu.VMEM((EARLY, 2, ncell // 16, nblocks * width), bf16),
+            pltpu.VMEM((4, 2, ncell // 16, nblocks * width), bf16),
             pltpu.VMEM((3, nblocks * width), f32),
-            dma((5,)), dma((2,)), dma((3, 4)), dma((3, 3)), dma((3, 8)),
-            dma((7,)), dma((7,)), dma((16,)), dma((16,)), dma, dma,
+            dma((5,)), dma((2,)), dma((2,)), dma((2, 3)), dma((2, 3)), dma((2,)), dma((2,)),
+            dma, dma, dma((3,)), dma((3,)), dma((3,)), dma((3,)), dma((3,)), dma((3,)), dma, dma,
         ],
         compiler_params=pltpu.CompilerParams(
             collective_id=0, has_side_effects=True, vmem_limit_bytes=56 << 20

time: 58.6 us -> 58.4 us (level)
  the two profiles are of different devices: /device:TPU:32 before, /device:TPU:17 now
where the time goes in v4:
time: 58.4 us; the launch traced here: 58.3 us
  Pallas kernels  57.5 us (98%)
  between operations  0.82 us (1%)
    pallas_call x1, Pallas kernels, on_device(): pl.pallas_call(exchange_and_far, out_shape=(jax.ShapeDtypeStruct((3, nblo...  39.3 us
    pallas_call x1, Pallas kernels, on_device(): pl.pallas_call(near_kernel, out_shape=jax.ShapeDtypeStruct((3, nblocks, w...  18.1 us

profile of v4, /device:TPU:17, one launch (start us, length us, event | category | flops | bytes accessed | tf_op | source)
XLA Modules:
  0.0 58.3 jit_solution(27392932446242644)
XLA Ops:
  0.7 39.3 %shard_map.55 = (f32[3,4096]{1,0:T(4,128)}, f32[2,12,296,128]{3,2,1,0:T(8,128)}) custom-call(f32[9,32,128]{2,1,0:T(8,128)} %bitcast.10, s32[1,32]{1,0:T(1,128)} %bitcast.12, f32[3,4096]{1,0:T(4,128)} %cc_hbm.1, s32[2,128]{1,0:T(2,128)} %bitcast.11, s32[1,1]{1,0:T(1,128)} %bitcast.7.live_hbm), custom_call_target="tpu_custom_call" | custom-call | tf_op jit(solution)/shard_map/pallas_call | solution.py:503
  40.0 18.1 %shard_map.56 = f32[3,32,128]{2,1,0:T(8,128)} custom-call(f32[7104,128]{1,0:T(8,128)} %bitcast.8, f32[24,296,128]{2,1,0:T(8,128)} %bitcast.9, f32[3,4096]{1,0:T(4,128)} %get-tuple-element.8.far_hbm), custom_call_target="tpu_custom_call" | custom-call | tf_op jit(solution)/shard_map/pallas_call | solution.py:540

commit v5 on v4

--- a/solution.py
+++ b/solution.py
@@ -129,11 +129,11 @@
     step = 1 + 2 * core
 
     def place(group, dz):
-        return win.at[core, dz] if group == 0 else win.at[core, pl.ds(4 + 2 * dz, 2)]
+        return win.at[core, dz] if group == 0 else win.at[core, 3 + group + 2 * dz]
 
     def spread(group, k):
         return send(
-            payload if group == 0 else place(1, 0), place(group, 4 - k),
+            payload if group == 0 else place(group, 0), place(group, 4 - k),
             z_send.at[group, k // 2], z_recv.at[group, 3 - k], along_z(k),
         )
 
@@ -143,9 +143,11 @@
             z_send.at[group, 2], z_recv.at[group, 1], along_z(step),
         )
 
-    def relay(group):
-        part = win.at[core, 0:4] if group == 0 else win.at[core, 4:12]
-        return send(part, part, r_send.at[group], r_recv.at[group], other_core)
+    relayed = [(0, 4), (4, 6), (6, 8), (10, 12), (8, 10)]
+
+    def relay(i):
+        part = win.at[core, relayed[i][0] : relayed[i][1]]
+        return send(part, part, r_send.at[i], r_recv.at[i], other_core)
 
     to_twin.start()
     after.start()
@@ -205,13 +207,26 @@
             m, lo, preferred_element_type=f32
         )
 
+    def make(k, carry):
+        early[k, 0], early[k, 1] = weights(region_of(k // 4, k % 4), False)
+        return carry
+
+    def use(k, carry):
+        acc[...] += product(k // 4, k % 4, early[k, 0], early[k, 1])
+        return carry
+
+    def whole(k, carry):
+        hi, lo = weights(region_of(k // 4, k % 4), False)
+        acc[...] += product(k // 4, k % 4, hi, lo)
+        return carry
+
     early[0, 0], early[0, 1] = weights(space, True)
 
     arrived(twin, twin_recv)
     pair_sum[...] = mine[...] + twin[...]
     for copy in to_z:
         copy.start()
-    early[1, 0], early[1, 1] = weights(region_of(0, 1), False)
+    lax.fori_loop(1, 3, make, 0)
 
     region = pair_sum[...]
     for k in range(3):
@@ -220,47 +235,46 @@
     moments[0, 0] = region
     for copy in to_y:
         copy.start()
-    early[2, 0], early[2, 1] = weights(region_of(0, 2), False)
+    for group in (1, 2):
+        arrived(place(group, 0), x_recv.at[group - 1])
+        for k in (1, 3):
+            spread(group, k).start()
+    relay(1).start()
+    lax.fori_loop(3, 5, make, 0)
 
     for k in range(3):
         arrived(moments.at[0, k + 1], y_recv.at[k])
     for copy in to_x:
         copy.start()
-    for k in range(2):
-        arrived(win.at[core, 4 + k], x_recv.at[k])
-    for k in (1, 3):
-        spread(1, k).start()
-    early[3, 0], early[3, 1] = weights(region_of(0, 3), False)
-
     for dz in (1, 3):
         arrived(place(0, dz), z_recv.at[0, dz - 1])
     forward(0).start()
+    lax.fori_loop(5, 7, make, 0)
+
+    for dz in (1, 3):
+        arrived(place(1, dz), z_recv.at[1, dz - 1])
+    forward(1).start()
+    lax.fori_loop(7, 8, make, 0)
     acc[...] = product(0, 0, early[0, 0], early[0, 1])
-    for k in range(1, 4):
-        acc[...] += product(0, k, early[k, 0], early[k, 1])
-
-    def later_chunk(k, carry):
-        dx, dy = k // 4, k % 4
-        hi, lo = weights(region_of(dx, dy), False)
-        acc[...] += product(dx, dy, hi, lo)
-        return carry
-
-    arrived(moments.at[1], m_recv.at[0])
-    lax.fori_loop(4, 6, later_chunk, 0)
+    lax.fori_loop(1, 4, use, 0)
+
+    for dz in (1, 3):
+        arrived(place(2, dz), z_recv.at[2, dz - 1])
+    forward(2).start()
+    relay(2).start()
+    relay(3).start()
     arrived(place(0, 2), z_recv.at[0, 1])
     own_copy.wait()
     relay(0).start()
-    lax.fori_loop(6, 8, later_chunk, 0)
+    arrived(moments.at[1], m_recv.at[0])
+    lax.fori_loop(4, 8, use, 0)
     arrived(moments.at[2], m_recv.at[1])
-    lax.fori_loop(8, 9, later_chunk, 0)
-    for dz in (1, 3):
-        arrived(place(1, dz), z_recv.at[1, dz - 1])
-    forward(1).start()
-    lax.fori_loop(9, 12, later_chunk, 0)
-    arrived(place(1, 2), z_recv.at[1, 1])
-    relay(1).start()
+    lax.fori_loop(8, 10, whole, 0)
+    for group in (1, 2):
+        arrived(place(group, 2), z_recv.at[group, 1])
+    relay(4).start()
     arrived(moments.at[3], m_recv.at[2])
-    lax.fori_loop(12, 16, later_chunk, 0)
+    lax.fori_loop(10, 16, whole, 0)
 
     grid = acc[0:9, :] + acc[16:25, :]
     line = flat[8:11, :]
@@ -272,15 +286,16 @@
     far_copy = pltpu.make_async_copy(far_ref, far_hbm, far_sem)
     far_copy.start()
 
-    arrived(win.at[1 - core, 0:4], r_recv.at[0])
-    arrived(win.at[1 - core, 4:12], r_recv.at[1])
+    for i, (lo, hi) in enumerate(relayed):
+        arrived(win.at[1 - core, lo:hi], r_recv.at[i])
     for copy in [to_twin, after, before] + to_z + to_y + to_x:
         copy.wait_send()
-    for group in range(2):
+    for group in range(3):
         for k in (1, 3):
             spread(group, k).wait_send()
         forward(group).wait_send()
-        relay(group).wait_send()
+    for i in range(len(relayed)):
+        relay(i).wait_send()
     far_copy.wait()
 
 
@@ -525,9 +540,9 @@
             pltpu.VMEM((ncell, 32), bf16),
             pltpu.VMEM((32, nblocks * width), bf16),
             pltpu.VMEM((32, nblocks * width), f32),
-            pltpu.VMEM((4, 2, ncell // 16, nblocks * width), bf16),
+            pltpu.VMEM((8, 2, ncell // 16, nblocks * width), bf16),
             pltpu.VMEM((3, nblocks * width), f32),
-            dma((5,)), dma((2,)), dma((2,)), dma((2, 3)), dma((2, 3)), dma((2,)), dma((2,)),
+            dma((5,)), dma((2,)), dma((2,)), dma((3, 3)), dma((3, 3)), dma((5,)), dma((5,)),
             dma, dma, dma((3,)), dma((3,)), dma((3,)), dma((3,)), dma((3,)), dma((3,)), dma, dma,
         ],
         compiler_params=pltpu.CompilerParams(

time: 58.4 us -> 55.6 us (0.952)
  the two profiles are of different devices: /device:TPU:17 before, /device:TPU:32 now
where the time goes in v5:
time: 55.6 us; the launch traced here: 55.5 us
  Pallas kernels  54.8 us (99%)
  between operations  0.66 us (1%)
    pallas_call x1, Pallas kernels, on_device(): pl.pallas_call(exchange_and_far, out_shape=(jax.ShapeDtypeStruct((3, nblo...  38.5 us
    pallas_call x1, Pallas kernels, on_device(): pl.pallas_call(near_kernel, out_shape=jax.ShapeDtypeStruct((3, nblocks, w...  16.4 us

profile of v5, /device:TPU:32, one launch (start us, length us, event | category | flops | bytes accessed | tf_op | source)
XLA Modules:
  0.0 55.5 jit_solution(13011656937226223046)
XLA Ops:
  0.7 38.5 %shard_map.55 = (f32[3,4096]{1,0:T(4,128)}, f32[2,12,296,128]{3,2,1,0:T(8,128)}) custom-call(f32[9,32,128]{2,1,0:T(8,128)} %bitcast.10, s32[1,32]{1,0:T(1,128)} %bitcast.12, f32[3,4096]{1,0:T(4,128)} %cc_hbm.1, s32[2,128]{1,0:T(2,128)} %bitcast.11, s32[1,1]{1,0:T(1,128)} %bitcast.7.live_hbm), custom_call_target="tpu_custom_call" | custom-call | tf_op jit(solution)/shard_map/pallas_call | solution.py:518
  39.1 16.4 %shard_map.56 = f32[3,32,128]{2,1,0:T(8,128)} custom-call(f32[7104,128]{1,0:T(8,128)} %bitcast.8, f32[24,296,128]{2,1,0:T(8,128)} %bitcast.9, f32[3,4096]{1,0:T(4,128)} %get-tuple-element.8.far_hbm), custom_call_target="tpu_custom_call" | custom-call | tf_op jit(solution)/shard_map/pallas_call | solution.py:555

commit v6 on v5

--- a/solution.py
+++ b/solution.py
@@ -11,6 +11,7 @@
 f32 = jnp.float32
 bf16 = jnp.bfloat16
 ROWS = 296
+RING = 6
 UNROLL = 8
 
 
@@ -207,26 +208,35 @@
             m, lo, preferred_element_type=f32
         )
 
-    def make(k, carry):
-        early[k, 0], early[k, 1] = weights(region_of(k // 4, k % 4), False)
+    def make(k):
+        early[k % RING, 0], early[k % RING, 1] = weights(region_of(k // 4, k % 4), False)
+
+    def use(k):
+        acc[...] += product(k // 4, k % 4, early[k % RING, 0], early[k % RING, 1])
+
+    def makes(k, carry):
+        make(k)
         return carry
 
-    def use(k, carry):
-        acc[...] += product(k // 4, k % 4, early[k, 0], early[k, 1])
-        return carry
-
-    def whole(k, carry):
-        hi, lo = weights(region_of(k // 4, k % 4), False)
-        acc[...] += product(k // 4, k % 4, hi, lo)
-        return carry
-
+    def one_use(k, behind):
+        use(k - behind)
+        make(k)
+        return behind
+
+    def two_uses(k, ahead):
+        use(2 * k - ahead)
+        use(2 * k - ahead + 1)
+        make(k)
+        return ahead
+
+    acc[...] = jnp.zeros_like(acc)
     early[0, 0], early[0, 1] = weights(space, True)
 
     arrived(twin, twin_recv)
     pair_sum[...] = mine[...] + twin[...]
     for copy in to_z:
         copy.start()
-    lax.fori_loop(1, 3, make, 0)
+    lax.fori_loop(1, 3, makes, 0)
 
     region = pair_sum[...]
     for k in range(3):
@@ -240,7 +250,7 @@
         for k in (1, 3):
             spread(group, k).start()
     relay(1).start()
-    lax.fori_loop(3, 5, make, 0)
+    lax.fori_loop(3, 5, makes, 0)
 
     for k in range(3):
         arrived(moments.at[0, k + 1], y_recv.at[k])
@@ -249,14 +259,12 @@
     for dz in (1, 3):
         arrived(place(0, dz), z_recv.at[0, dz - 1])
     forward(0).start()
-    lax.fori_loop(5, 7, make, 0)
+    lax.fori_loop(5, 7, one_use, 5)
 
     for dz in (1, 3):
         arrived(place(1, dz), z_recv.at[1, dz - 1])
     forward(1).start()
-    lax.fori_loop(7, 8, make, 0)
-    acc[...] = product(0, 0, early[0, 0], early[0, 1])
-    lax.fori_loop(1, 4, use, 0)
+    lax.fori_loop(7, 9, one_use, 5)
 
     for dz in (1, 3):
         arrived(place(2, dz), z_recv.at[2, dz - 1])
@@ -267,14 +275,18 @@
     own_copy.wait()
     relay(0).start()
     arrived(moments.at[1], m_recv.at[0])
-    lax.fori_loop(4, 8, use, 0)
-    arrived(moments.at[2], m_recv.at[1])
-    lax.fori_loop(8, 10, whole, 0)
+    lax.fori_loop(9, 11, two_uses, 14)
+
     for group in (1, 2):
         arrived(place(group, 2), z_recv.at[group, 1])
     relay(4).start()
+    arrived(moments.at[2], m_recv.at[1])
+    lax.fori_loop(11, 12, two_uses, 14)
+    lax.fori_loop(12, 13, one_use, 2)
     arrived(moments.at[3], m_recv.at[2])
-    lax.fori_loop(10, 16, whole, 0)
+    lax.fori_loop(13, 16, one_use, 2)
+    use(14)
+    use(15)
 
     grid = acc[0:9, :] + acc[16:25, :]
     line = flat[8:11, :]
@@ -300,20 +312,29 @@
 
 
 def arrangement():
-    r = lax.broadcasted_iota(jnp.int32, (64, 384), 0)
-    q = lax.broadcasted_iota(jnp.int32, (64, 384), 1)
+    r = lax.broadcasted_iota(jnp.int32, (64, 256), 0)
+    q = lax.broadcasted_iota(jnp.int32, (64, 256), 1)
     kind, col = q // 128, q % 128
     group, line = col // 16, col % 16
     mate = jnp.where(group < 3, group, jnp.where(group < 5, group - 3, 0))
-    dist = (kind == 0) & (group < 6) & (line < 3) & (r == mate * 16 + line)
+    same = (group < 6) & (r == mate * 16 + line)
+    dist = (kind == 0) & same & (line < 3)
     extra = (kind == 0) & (group == 6) & (
         ((line < 3) & (r == 48 + 3 + line)) | ((line >= 3) & (line < 6) & (r == 48))
     )
-    burg_line = (kind == 1) & (group < 6) & (line >= 3) & (line < 6) & (r == mate * 16 + line + 3)
-    line_burg = (kind == 2) & (group < 6) & (line >= 6) & (line < 9) & (r == mate * 16 + line - 3)
-    return jnp.where(
-        dist, -2.0, jnp.where(extra | burg_line | line_burg, 1.0, 0.0)
-    ).astype(bf16)
+    couple = (kind == 1) & same & (line >= 3) & (line < 12)
+    return jnp.where(dist, -2.0, jnp.where(extra | couple, 1.0, 0.0)).astype(bf16)
+
+
+def block_rows(ref, row, origin, first, second):
+    row16 = lax.broadcasted_iota(jnp.int32, (16, 128), 0)
+    u = [ref[pl.ds(row + first + k, 1), :] for k in range(3)]
+    v = [ref[pl.ds(row + second + k, 1), :] for k in range(3)]
+    left = jnp.where(row16 < 6, u[0], jnp.where(row16 < 9, u[1], u[2]))
+    place = row16 % 3
+    right = jnp.where(place == 0, v[0], jnp.where(place == 1, v[1], v[2]))
+    both = jnp.where(row16 < 12, left * right, 0.0)
+    return jnp.where(row16 < 3, ref[pl.ds(row, 16), :] - origin, both)
 
 
 def split_rows(x, plus):
@@ -419,7 +440,7 @@
 
 def near_kernel(
     win_hbm, pair_hbm, far_hbm, out_ref,
-    win_ref, pair_ref, own_ref, far_ref, feats, arrange, acc, hots, listed, table, sem, in_sem,
+    win_ref, pair_ref, own_ref, far_ref, feats, arrange, unit, acc, hots, listed, table, sem, in_sem,
 ):
     space, sub = lax.axis_index("space"), lax.axis_index("sub")
     nblocks = out_ref.shape[1]
@@ -439,18 +460,19 @@
 
     arrange[...] = arrangement()
     acc[...] = jnp.zeros_like(acc)
+    row16 = lax.broadcasted_iota(jnp.int32, (16, 128), 0)
     for q in range(0, nblocks, 8):
-        x = jnp.concatenate(
-            [
-                jnp.concatenate(
-                    split_rows(own_ref[9 * g : 9 * g + 16, :] - origin, 0.25), axis=0
-                )
-                for g in range(q, q + 8)
-            ],
-            axis=1,
-        )
+        parts = []
+        for g in range(q, q + 8):
+            x = block_rows(own_ref, 9 * g, origin, 6, 3)
+            size = jnp.max(jnp.where(row16 < 3, 0.0, jnp.abs(x)), axis=0, keepdims=True)
+            size = jnp.maximum(jnp.max(size, axis=1, keepdims=True), 1e-30)
+            unit[g : g + 1, :] = jnp.broadcast_to(size, (1, 128))
+            x = jnp.where(row16 < 3, x, x * (1.0 / size))
+            parts.append(jnp.concatenate(split_rows(x, 0.25), axis=0))
         f = lax.dot_general(
-            x, arrange[...], (((0,), (0,)), ((), ())), preferred_element_type=f32
+            jnp.concatenate(parts, axis=1), arrange[...], (((0,), (0,)), ((), ())),
+            preferred_element_type=f32,
         )
         feats[q * 128 : q * 128 + 1024, :] = f.astype(bf16)
 
@@ -472,20 +494,20 @@
             for v in range(2):
                 other = table[row, col + v]
                 alive.append(jnp.where(inside, table[row + 2, col + v], 0).astype(f32))
-                a, b, c, ext = split_rows(win_ref[pl.ds(other, 16), :] - origin, 0.0)
+                a, b, c, ext = split_rows(block_rows(win_ref, other, origin, 3, 6), 0.0)
                 rhs.append(
                     jnp.concatenate(
                         [a, a, a, b, b, c, ext, jnp.zeros((16, 128), bf16)], axis=0
                     )
                 )
             f = feats[pl.ds(pl.multiple_of(own * 128, 128), 128), :]
-            f = jnp.concatenate([f[:, 0:128], f[:, 128:256], f[:, 256:384]], axis=0)
+            f = jnp.concatenate([f[:, 0:128], f[:, 128:256]], axis=0)
             work.append((own, jnp.where(half, alive[0], alive[1]), f, jnp.concatenate(rhs, axis=1)))
         outs = [jnp.dot(f, rhs, preferred_element_type=f32) for _, _, f, rhs in work]
         sums = []
         for (own, live, _, rhs), out in zip(work, outs):
             inv = lax.rsqrt(jnp.maximum(out[0:128], 0.25))
-            g = (inv * inv) * (inv * live) * (out[128:256] * out[256:384])
+            g = (inv * inv) * (inv * live) * out[128:256]
             hi = g.astype(bf16)
             lo = (g - hi.astype(f32)).astype(bf16)
             lhs = jnp.concatenate([rhs[0:16], rhs[48:64], rhs[80:112]], axis=0)
@@ -503,7 +525,8 @@
     for g in range(nblocks):
         p = own_ref[9 * g : 9 * g + 16, :] - origin
         t = acc[g]
-        force = far_ref[0:3, g * 128 : g * 128 + 128] + p[0:3] * t[3:4] - t[0:3]
+        near = (p[0:3] * t[3:4] - t[0:3]) * unit[g : g + 1, :]
+        force = far_ref[0:3, g * 128 : g * 128 + 128] + near
         for a in range(3):
             out_ref[a, g : g + 1, :] = force[a : a + 1]
 
@@ -540,7 +563,7 @@
             pltpu.VMEM((ncell, 32), bf16),
             pltpu.VMEM((32, nblocks * width), bf16),
             pltpu.VMEM((32, nblocks * width), f32),
-            pltpu.VMEM((8, 2, ncell // 16, nblocks * width), bf16),
+            pltpu.VMEM((RING, 2, ncell // 16, nblocks * width), bf16),
             pltpu.VMEM((3, nblocks * width), f32),
             dma((5,)), dma((2,)), dma((2,)), dma((3, 3)), dma((3, 3)), dma((5,)), dma((5,)),
             dma, dma, dma((3,)), dma((3,)), dma((3,)), dma((3,)), dma((3,)), dma((3,)), dma, dma,
@@ -562,8 +585,9 @@
             pltpu.VMEM((24, 8, width), f32),
             pltpu.VMEM((ROWS, width), f32),
             pltpu.VMEM((3, nblocks * width), f32),
-            pltpu.VMEM((nblocks * width, 384), bf16),
-            pltpu.VMEM((64, 384), bf16),
+            pltpu.VMEM((nblocks * width, 256), bf16),
+            pltpu.VMEM((64, 256), bf16),
+            pltpu.VMEM((nblocks, width), f32),
             pltpu.VMEM((nblocks, 16, width), f32),
             pltpu.VMEM((25 * 32, width), f32),
             pltpu.VMEM((8, width), jnp.int32),

time: 55.6 us -> 55.4 us (level)
  the two profiles are of different devices: /device:TPU:32 before, /device:TPU:48 now
where the time goes in v6:
time: 55.4 us; the launch traced here: 55.3 us
  Pallas kernels  54.5 us (98%)
  between operations  0.82 us (1%)
    pallas_call x1, Pallas kernels, on_device(): pl.pallas_call(exchange_and_far, out_shape=(jax.ShapeDtypeStruct((3, nblo...  37.9 us
    pallas_call x1, Pallas kernels, on_device(): pl.pallas_call(near_kernel, out_shape=jax.ShapeDtypeStruct((3, nblocks, w...  16.6 us

profile of v6, /device:TPU:48, one launch (start us, length us, event | category | flops | bytes accessed | tf_op | source)
XLA Modules:
  0.0 55.3 jit_solution(13129953656824096480)
XLA Ops:
  0.7 37.9 %shard_map.55 = (f32[3,4096]{1,0:T(4,128)}, f32[2,12,296,128]{3,2,1,0:T(8,128)}) custom-call(f32[9,32,128]{2,1,0:T(8,128)} %bitcast.10, s32[1,32]{1,0:T(1,128)} %bitcast.12, f32[3,4096]{1,0:T(4,128)} %cc_hbm.1, s32[2,128]{1,0:T(2,128)} %bitcast.11, s32[1,1]{1,0:T(1,128)} %bitcast.7.live_hbm), custom_call_target="tpu_custom_call" | custom-call | tf_op jit(solution)/shard_map/pallas_call | solution.py:541
  38.6 16.6 %shard_map.56 = f32[3,32,128]{2,1,0:T(8,128)} custom-call(f32[7104,128]{1,0:T(8,128)} %bitcast.8, f32[24,296,128]{2,1,0:T(8,128)} %bitcast.9, f32[3,4096]{1,0:T(4,128)} %get-tuple-element.8.far_hbm), custom_call_target="tpu_custom_call" | custom-call | tf_op jit(solution)/shard_map/pallas_call | solution.py:578

commit v7 on v6

--- a/solution.py
+++ b/solution.py
@@ -11,8 +11,7 @@
 f32 = jnp.float32
 bf16 = jnp.bfloat16
 ROWS = 296
-RING = 6
-UNROLL = 8
+UNROLL = 12
 
 
 def three(x):
@@ -208,35 +207,25 @@
             m, lo, preferred_element_type=f32
         )
 
-    def make(k):
-        early[k % RING, 0], early[k % RING, 1] = weights(region_of(k // 4, k % 4), False)
-
-    def use(k):
-        acc[...] += product(k // 4, k % 4, early[k % RING, 0], early[k % RING, 1])
-
-    def makes(k, carry):
-        make(k)
+    def make(k, carry):
+        early[k, 0], early[k, 1] = weights(region_of(0, k), False)
         return carry
 
-    def one_use(k, behind):
-        use(k - behind)
-        make(k)
-        return behind
-
-    def two_uses(k, ahead):
-        use(2 * k - ahead)
-        use(2 * k - ahead + 1)
-        make(k)
-        return ahead
-
-    acc[...] = jnp.zeros_like(acc)
+    def two(j, carry):
+        k = 2 * j
+        dx, dy = k // 4, k % 4
+        hi, lo = weights(region_of(dx, dy), False)
+        hi2, lo2 = weights(region_of(dx, dy + 1), False)
+        acc[...] += product(dx, dy, hi, lo) + product(dx, dy + 1, hi2, lo2)
+        return carry
+
     early[0, 0], early[0, 1] = weights(space, True)
 
     arrived(twin, twin_recv)
     pair_sum[...] = mine[...] + twin[...]
     for copy in to_z:
         copy.start()
-    lax.fori_loop(1, 3, makes, 0)
+    lax.fori_loop(1, 2, make, 0)
 
     region = pair_sum[...]
     for k in range(3):
@@ -245,12 +234,13 @@
     moments[0, 0] = region
     for copy in to_y:
         copy.start()
+    lax.fori_loop(2, 4, make, 0)
     for group in (1, 2):
         arrived(place(group, 0), x_recv.at[group - 1])
         for k in (1, 3):
             spread(group, k).start()
     relay(1).start()
-    lax.fori_loop(3, 5, makes, 0)
+    acc[...] = product(0, 0, early[0, 0], early[0, 1])
 
     for k in range(3):
         arrived(moments.at[0, k + 1], y_recv.at[k])
@@ -259,13 +249,18 @@
     for dz in (1, 3):
         arrived(place(0, dz), z_recv.at[0, dz - 1])
     forward(0).start()
-    lax.fori_loop(5, 7, one_use, 5)
-
+    acc[...] += (
+        product(0, 1, early[1, 0], early[1, 1])
+        + product(0, 2, early[2, 0], early[2, 1])
+        + product(0, 3, early[3, 0], early[3, 1])
+    )
+
+    arrived(moments.at[1], m_recv.at[0])
+    lax.fori_loop(2, 3, two, 0)
     for dz in (1, 3):
         arrived(place(1, dz), z_recv.at[1, dz - 1])
     forward(1).start()
-    lax.fori_loop(7, 9, one_use, 5)
-
+    lax.fori_loop(3, 4, two, 0)
     for dz in (1, 3):
         arrived(place(2, dz), z_recv.at[2, dz - 1])
     forward(2).start()
@@ -274,19 +269,13 @@
     arrived(place(0, 2), z_recv.at[0, 1])
     own_copy.wait()
     relay(0).start()
-    arrived(moments.at[1], m_recv.at[0])
-    lax.fori_loop(9, 11, two_uses, 14)
-
+    arrived(moments.at[2], m_recv.at[1])
+    lax.fori_loop(4, 6, two, 0)
     for group in (1, 2):
         arrived(place(group, 2), z_recv.at[group, 1])
     relay(4).start()
-    arrived(moments.at[2], m_recv.at[1])
-    lax.fori_loop(11, 12, two_uses, 14)
-    lax.fori_loop(12, 13, one_use, 2)
     arrived(moments.at[3], m_recv.at[2])
-    lax.fori_loop(13, 16, one_use, 2)
-    use(14)
-    use(15)
+    lax.fori_loop(6, 8, two, 0)
 
     grid = acc[0:9, :] + acc[16:25, :]
     line = flat[8:11, :]
@@ -312,8 +301,8 @@
 
 
 def arrangement():
-    r = lax.broadcasted_iota(jnp.int32, (64, 256), 0)
-    q = lax.broadcasted_iota(jnp.int32, (64, 256), 1)
+    q = lax.broadcasted_iota(jnp.int32, (256, 64), 0)
+    r = lax.broadcasted_iota(jnp.int32, (256, 64), 1)
     kind, col = q // 128, q % 128
     group, line = col // 16, col % 16
     mate = jnp.where(group < 3, group, jnp.where(group < 5, group - 3, 0))
@@ -470,14 +459,14 @@
             unit[g : g + 1, :] = jnp.broadcast_to(size, (1, 128))
             x = jnp.where(row16 < 3, x, x * (1.0 / size))
             parts.append(jnp.concatenate(split_rows(x, 0.25), axis=0))
-        f = lax.dot_general(
-            jnp.concatenate(parts, axis=1), arrange[...], (((0,), (0,)), ((), ())),
-            preferred_element_type=f32,
-        )
-        feats[q * 128 : q * 128 + 1024, :] = f.astype(bf16)
+        f = jnp.dot(
+            arrange[...], jnp.concatenate(parts, axis=1), preferred_element_type=f32
+        ).astype(bf16)
+        for g in range(8):
+            feats[q + g, :, 0:128] = f[0:128, g * 128 : g * 128 + 128]
+            feats[q + g, :, 128:256] = f[128:256, g * 128 : g * 128 + 128]
 
     win_in.wait()
-    half = lax.broadcasted_iota(jnp.int32, (1, 256), 1) < 128
     top = lax.broadcasted_iota(jnp.int32, (16, 128), 0) < 3
 
     def items(step, carry):
@@ -500,20 +489,23 @@
                         [a, a, a, b, b, c, ext, jnp.zeros((16, 128), bf16)], axis=0
                     )
                 )
-            f = feats[pl.ds(pl.multiple_of(own * 128, 128), 128), :]
-            f = jnp.concatenate([f[:, 0:128], f[:, 128:256]], axis=0)
-            work.append((own, jnp.where(half, alive[0], alive[1]), f, jnp.concatenate(rhs, axis=1)))
-        outs = [jnp.dot(f, rhs, preferred_element_type=f32) for _, _, f, rhs in work]
+            work.append((own, alive, jnp.concatenate(rhs, axis=1)))
+        outs = [
+            lax.dot_general(
+                rhs, feats[own], (((0,), (0,)), ((), ())), preferred_element_type=f32
+            )
+            for own, _, rhs in work
+        ]
         sums = []
-        for (own, live, _, rhs), out in zip(work, outs):
-            inv = lax.rsqrt(jnp.maximum(out[0:128], 0.25))
-            g = (inv * inv) * (inv * live) * out[128:256]
+        for (own, alive, rhs), out in zip(work, outs):
+            inv = lax.rsqrt(jnp.maximum(out[:, 0:128], 0.25))
+            live = jnp.concatenate([inv[0:128] * alive[0], inv[128:256] * alive[1]], axis=0)
+            g = (inv * inv) * live * out[:, 128:256]
             hi = g.astype(bf16)
             lo = (g - hi.astype(f32)).astype(bf16)
             lhs = jnp.concatenate([rhs[0:16], rhs[48:64], rhs[80:112]], axis=0)
-            dims = (((1,), (1,)), ((), ()))
-            r = lax.dot_general(lhs, hi, dims, preferred_element_type=f32)
-            r = r + lax.dot_general(lhs, lo, dims, preferred_element_type=f32)
+            r = jnp.dot(lhs, hi, preferred_element_type=f32)
+            r = r + jnp.dot(lhs, lo, preferred_element_type=f32)
             sums.append((own, jnp.where(top, r[0:16] + r[16:32] + r[32:48], r[48:49])))
         for own, r in sums:
             acc[own] += r
@@ -563,7 +555,7 @@
             pltpu.VMEM((ncell, 32), bf16),
             pltpu.VMEM((32, nblocks * width), bf16),
             pltpu.VMEM((32, nblocks * width), f32),
-            pltpu.VMEM((RING, 2, ncell // 16, nblocks * width), bf16),
+            pltpu.VMEM((4, 2, ncell // 16, nblocks * width), bf16),
             pltpu.VMEM((3, nblocks * width), f32),
             dma((5,)), dma((2,)), dma((2,)), dma((3, 3)), dma((3, 3)), dma((5,)), dma((5,)),
             dma, dma, dma((3,)), dma((3,)), dma((3,)), dma((3,)), dma((3,)), dma((3,)), dma, dma,
@@ -585,8 +577,8 @@
             pltpu.VMEM((24, 8, width), f32),
             pltpu.VMEM((ROWS, width), f32),
             pltpu.VMEM((3, nblocks * width), f32),
-            pltpu.VMEM((nblocks * width, 256), bf16),
-            pltpu.VMEM((64, 256), bf16),
+            pltpu.VMEM((nblocks, 128, 256), bf16),
+            pltpu.VMEM((256, 64), bf16),
             pltpu.VMEM((nblocks, width), f32),
             pltpu.VMEM((nblocks, 16, width), f32),
             pltpu.VMEM((25 * 32, width), f32),

time: 55.4 us -> 51 us (0.921)
  the two profiles are of different devices: /device:TPU:48 before, /device:TPU:32 now
where the time goes in v7:
time: 51 us; the launch traced here: 50.4 us
  Pallas kernels  49.6 us (97%)
  between operations  0.84 us (2%)
    pallas_call x1, Pallas kernels, on_device(): pl.pallas_call(exchange_and_far, out_shape=(jax.ShapeDtypeStruct((3, nblo...  35.8 us
    pallas_call x1, Pallas kernels, on_device(): pl.pallas_call(near_kernel, out_shape=jax.ShapeDtypeStruct((3, nblocks, w...  13.8 us

profile of v7, /device:TPU:32, one launch (start us, length us, event | category | flops | bytes accessed | tf_op | source)
XLA Modules:
  0.0 50.4 jit_solution(16228034239987874846)
XLA Ops:
  0.7 35.8 %shard_map.55 = (f32[3,4096]{1,0:T(4,128)}, f32[2,12,296,128]{3,2,1,0:T(8,128)}) custom-call(f32[9,32,128]{2,1,0:T(8,128)} %bitcast.10, s32[1,32]{1,0:T(1,128)} %bitcast.12, f32[3,4096]{1,0:T(4,128)} %cc_hbm.1, s32[2,128]{1,0:T(2,128)} %bitcast.11, s32[1,1]{1,0:T(1,128)} %bitcast.7.live_hbm), custom_call_target="tpu_custom_call" | custom-call | tf_op jit(solution)/shard_map/pallas_call | solution.py:533
  36.5 13.8 %shard_map.56 = f32[3,32,128]{2,1,0:T(8,128)} custom-call(f32[7104,128]{1,0:T(8,128)} %bitcast.8, f32[24,296,128]{2,1,0:T(8,128)} %bitcast.9, f32[3,4096]{1,0:T(4,128)} %get-tuple-element.8.far_hbm), custom_call_target="tpu_custom_call" | custom-call | tf_op jit(solution)/shard_map/pallas_call | solution.py:570

commit v8 on v7

--- a/solution.py
+++ b/solution.py
@@ -30,24 +30,24 @@
 ):
     space = lax.axis_index("space")
     sub = lax.axis_index("sub")
-    y, x = space // 4, space % 4
-    z, core = sub // 2, sub % 2
+    y, x = lax.div(space, 4), lax.rem(space, 4)
+    z, core = lax.div(sub, 2), lax.rem(sub, 2)
     nblocks = seg_ref.shape[1]
     ncell = cc_ref.shape[1]
     per = ncell // 16
     other_core = (space, z * 2 + 1 - core)
 
     def along_z(k):
-        return (space, (z + k) % 4 * 2 + core)
+        return (space, lax.rem(z + k, 4) * 2 + core)
 
     def along_y(k):
-        return ((y + k) % 4 * 4 + x, sub)
+        return (lax.rem(y + k, 4) * 4 + x, sub)
 
     def along_x(k):
-        return (y * 4 + (x + k) % 4, sub)
+        return (y * 4 + lax.rem(x + k, 4), sub)
 
     def along_space(k):
-        return ((space + k) % 16, sub)
+        return (lax.rem(space + k, 16), sub)
 
     ins = [
         pltpu.make_async_copy(src, dst, in_sem.at[i])
@@ -128,22 +128,22 @@
     before = send(payload, win.at[core, 5], x_send.at[1], x_recv.at[1], along_space(15))
     step = 1 + 2 * core
 
-    def place(group, dz):
-        return win.at[core, dz] if group == 0 else win.at[core, 3 + group + 2 * dz]
-
-    def spread(group, k):
+    def place(group, j):
+        return win.at[core, j] if group == 0 else win.at[core, pl.ds(4 + 2 * j, 2)]
+
+    def spread(group, j):
         return send(
-            payload if group == 0 else place(group, 0), place(group, 4 - k),
-            z_send.at[group, k // 2], z_recv.at[group, 3 - k], along_z(k),
+            payload if group == 0 else place(1, 0), place(group, 2 - j),
+            z_send.at[group, j], z_recv.at[group, 1 - j], along_z(1 + 2 * j),
         )
 
     def forward(group):
         return send(
-            place(group, 4 - step), place(group, 2),
-            z_send.at[group, 2], z_recv.at[group, 1], along_z(step),
+            place(group, 2 - core), place(group, 3),
+            z_send.at[group, 2], z_recv.at[group, 2], along_z(step),
         )
 
-    relayed = [(0, 4), (4, 6), (6, 8), (10, 12), (8, 10)]
+    relayed = [(0, 4), (4, 10), (10, 12)]
 
     def relay(i):
         part = win.at[core, relayed[i][0] : relayed[i][1]]
@@ -152,8 +152,8 @@
     to_twin.start()
     after.start()
     before.start()
-    for k in (1, 3):
-        spread(0, k).start()
+    for j in (0, 1):
+        spread(0, j).start()
 
     for g in range(nblocks):
         lanes = slice(g * 128, g * 128 + 128)
@@ -177,7 +177,7 @@
     ).astype(bf16)
 
     def region_of(dx, dy):
-        return (y + dy) % 4 * 4 + (x + dx) % 4
+        return lax.rem(y + dy, 4) * 4 + lax.rem(x + dx, 4)
 
     def weights(region, first):
         at = pl.multiple_of(region * per, 256)
@@ -213,7 +213,7 @@
 
     def two(j, carry):
         k = 2 * j
-        dx, dy = k // 4, k % 4
+        dx, dy = lax.div(k, 4), lax.rem(k, 4)
         hi, lo = weights(region_of(dx, dy), False)
         hi2, lo2 = weights(region_of(dx, dy + 1), False)
         acc[...] += product(dx, dy, hi, lo) + product(dx, dy + 1, hi2, lo2)
@@ -235,19 +235,18 @@
     for copy in to_y:
         copy.start()
     lax.fori_loop(2, 4, make, 0)
-    for group in (1, 2):
-        arrived(place(group, 0), x_recv.at[group - 1])
-        for k in (1, 3):
-            spread(group, k).start()
-    relay(1).start()
+    for j in (0, 1):
+        arrived(win.at[core, 4 + j], x_recv.at[j])
+    for j in (0, 1):
+        spread(1, j).start()
     acc[...] = product(0, 0, early[0, 0], early[0, 1])
 
     for k in range(3):
         arrived(moments.at[0, k + 1], y_recv.at[k])
     for copy in to_x:
         copy.start()
-    for dz in (1, 3):
-        arrived(place(0, dz), z_recv.at[0, dz - 1])
+    for j in (0, 1):
+        arrived(place(0, j + 1), z_recv.at[0, j])
     forward(0).start()
     acc[...] += (
         product(0, 1, early[1, 0], early[1, 1])
@@ -256,24 +255,18 @@
     )
 
     arrived(moments.at[1], m_recv.at[0])
-    lax.fori_loop(2, 3, two, 0)
-    for dz in (1, 3):
-        arrived(place(1, dz), z_recv.at[1, dz - 1])
+    lax.fori_loop(2, 4, two, 0)
+    for j in (0, 1):
+        arrived(place(1, j + 1), z_recv.at[1, j])
     forward(1).start()
-    lax.fori_loop(3, 4, two, 0)
-    for dz in (1, 3):
-        arrived(place(2, dz), z_recv.at[2, dz - 1])
-    forward(2).start()
-    relay(2).start()
-    relay(3).start()
-    arrived(place(0, 2), z_recv.at[0, 1])
+    relay(1).start()
+    arrived(place(0, 3), z_recv.at[0, 2])
     own_copy.wait()
     relay(0).start()
     arrived(moments.at[2], m_recv.at[1])
     lax.fori_loop(4, 6, two, 0)
-    for group in (1, 2):
-        arrived(place(group, 2), z_recv.at[group, 1])
-    relay(4).start()
+    arrived(place(1, 3), z_recv.at[1, 2])
+    relay(2).start()
     arrived(moments.at[3], m_recv.at[2])
     lax.fori_loop(6, 8, two, 0)
 
@@ -291,9 +284,9 @@
         arrived(win.at[1 - core, lo:hi], r_recv.at[i])
     for copy in [to_twin, after, before] + to_z + to_y + to_x:
         copy.wait_send()
-    for group in range(3):
-        for k in (1, 3):
-            spread(group, k).wait_send()
+    for group in range(2):
+        for j in (0, 1):
+            spread(group, j).wait_send()
         forward(group).wait_send()
     for i in range(len(relayed)):
         relay(i).wait_send()
@@ -361,6 +354,7 @@
     ahead = jnp.where(ahead < -8, ahead + 16.0, jnp.where(ahead > 8, ahead - 16.0, ahead))
     dz = their_z - (sub // 2).astype(f32)
     dz = jnp.where(dz < 0, dz + 4.0, dz)
+    dz = jnp.where(dz == 3, 2.0, jnp.where(dz == 2, 3.0, dz))
     dev = (their_sub - 2.0 * their_z) * 12.0 + jnp.where(
         ahead == 0, dz, 4.0 + 2.0 * dz + (ahead > 0).astype(f32)
     )
@@ -475,8 +469,8 @@
             k = (step * UNROLL + u) * 2
             inside = k < count
             k = jnp.minimum(k, count - 2)
-            row = k // 128 * 8
-            col = k % 128
+            row = lax.div(k, 128) * 8
+            col = lax.rem(k, 128)
             own = table[row + 1, col]
             rhs = []
             alive = []
@@ -557,7 +551,7 @@
             pltpu.VMEM((32, nblocks * width), f32),
             pltpu.VMEM((4, 2, ncell // 16, nblocks * width), bf16),
             pltpu.VMEM((3, nblocks * width), f32),
-            dma((5,)), dma((2,)), dma((2,)), dma((3, 3)), dma((3, 3)), dma((5,)), dma((5,)),
+            dma((5,)), dma((2,)), dma((2,)), dma((2, 3)), dma((2, 3)), dma((3,)), dma((3,)),
             dma, dma, dma((3,)), dma((3,)), dma((3,)), dma((3,)), dma((3,)), dma((3,)), dma, dma,
         ],
         compiler_params=pltpu.CompilerParams(

time: 51 us -> 51.8 us (1.016)
  no operation moved by 1% of the time
where the time goes in v8:
time: 51.8 us; the launch traced here: 50.9 us
  Pallas kernels  50.1 us (97%)
  between operations  0.82 us (2%)
    pallas_call x1, Pallas kernels, on_device(): pl.pallas_call(exchange_and_far, out_shape=(jax.ShapeDtypeStruct((3, nblo...  36.2 us
    pallas_call x1, Pallas kernels, on_device(): pl.pallas_call(near_kernel, out_shape=jax.ShapeDtypeStruct((3, nblocks, w...  14 us

profile of v8, /device:TPU:32, one launch (start us, length us, event | category | flops | bytes accessed | tf_op | source)
XLA Modules:
  0.0 50.9 jit_solution(15763636090284426294)
XLA Ops:
  0.7 36.2 %shard_map.55 = (f32[3,4096]{1,0:T(4,128)}, f32[2,12,296,128]{3,2,1,0:T(8,128)}) custom-call(f32[9,32,128]{2,1,0:T(8,128)} %bitcast.10, s32[1,32]{1,0:T(1,128)} %bitcast.12, f32[3,4096]{1,0:T(4,128)} %cc_hbm.1, s32[2,128]{1,0:T(2,128)} %bitcast.11, s32[1,1]{1,0:T(1,128)} %bitcast.7.live_hbm), custom_call_target="tpu_custom_call" | custom-call | tf_op jit(solution)/shard_map/pallas_call | solution.py:527
  36.8 14.0 %shard_map.56 = f32[3,32,128]{2,1,0:T(8,128)} custom-call(f32[7104,128]{1,0:T(8,128)} %bitcast.8, f32[24,296,128]{2,1,0:T(8,128)} %bitcast.9, f32[3,4096]{1,0:T(4,128)} %get-tuple-element.8.far_hbm), custom_call_target="tpu_custom_call" | custom-call | tf_op jit(solution)/shard_map/pallas_call | solution.py:564

commit v9 on v8

--- a/solution.py
+++ b/solution.py
@@ -129,11 +129,11 @@
     step = 1 + 2 * core
 
     def place(group, j):
-        return win.at[core, j] if group == 0 else win.at[core, pl.ds(4 + 2 * j, 2)]
+        return win.at[core, j if group == 0 else 3 + group + 2 * j]
 
     def spread(group, j):
         return send(
-            payload if group == 0 else place(1, 0), place(group, 2 - j),
+            payload if group == 0 else place(group, 0), place(group, 2 - j),
             z_send.at[group, j], z_recv.at[group, 1 - j], along_z(1 + 2 * j),
         )
 
@@ -152,8 +152,6 @@
     to_twin.start()
     after.start()
     before.start()
-    for j in (0, 1):
-        spread(0, j).start()
 
     for g in range(nblocks):
         lanes = slice(g * 128, g * 128 + 128)
@@ -208,7 +206,7 @@
         )
 
     def make(k, carry):
-        early[k, 0], early[k, 1] = weights(region_of(0, k), False)
+        early[k, 0], early[k, 1] = weights(region_of(lax.div(k, 4), lax.rem(k, 4)), False)
         return carry
 
     def two(j, carry):
@@ -225,7 +223,9 @@
     pair_sum[...] = mine[...] + twin[...]
     for copy in to_z:
         copy.start()
-    lax.fori_loop(1, 2, make, 0)
+    for j in (0, 1):
+        spread(0, j).start()
+    lax.fori_loop(1, 4, make, 0)
 
     region = pair_sum[...]
     for k in range(3):
@@ -234,11 +234,11 @@
     moments[0, 0] = region
     for copy in to_y:
         copy.start()
-    lax.fori_loop(2, 4, make, 0)
-    for j in (0, 1):
-        arrived(win.at[core, 4 + j], x_recv.at[j])
-    for j in (0, 1):
-        spread(1, j).start()
+    for group in (1, 2):
+        arrived(place(group, 0), x_recv.at[group - 1])
+        for j in (0, 1):
+            spread(group, j).start()
+    lax.fori_loop(4, 6, make, 0)
     acc[...] = product(0, 0, early[0, 0], early[0, 1])
 
     for k in range(3):
@@ -255,20 +255,27 @@
     )
 
     arrived(moments.at[1], m_recv.at[0])
-    lax.fori_loop(2, 4, two, 0)
+    acc[...] += product(1, 0, early[4, 0], early[4, 1]) + product(1, 1, early[5, 0], early[5, 1])
     for j in (0, 1):
         arrived(place(1, j + 1), z_recv.at[1, j])
     forward(1).start()
+    lax.fori_loop(3, 4, two, 0)
+    arrived(moments.at[2], m_recv.at[1])
+    lax.fori_loop(4, 5, two, 0)
+    for j in (0, 1):
+        arrived(place(2, j + 1), z_recv.at[2, j])
+    forward(2).start()
     relay(1).start()
     arrived(place(0, 3), z_recv.at[0, 2])
     own_copy.wait()
     relay(0).start()
-    arrived(moments.at[2], m_recv.at[1])
-    lax.fori_loop(4, 6, two, 0)
-    arrived(place(1, 3), z_recv.at[1, 2])
+    lax.fori_loop(5, 6, two, 0)
+    arrived(moments.at[3], m_recv.at[2])
+    lax.fori_loop(6, 7, two, 0)
+    for group in (1, 2):
+        arrived(place(group, 3), z_recv.at[group, 2])
     relay(2).start()
-    arrived(moments.at[3], m_recv.at[2])
-    lax.fori_loop(6, 8, two, 0)
+    lax.fori_loop(7, 8, two, 0)
 
     grid = acc[0:9, :] + acc[16:25, :]
     line = flat[8:11, :]
@@ -284,7 +291,7 @@
         arrived(win.at[1 - core, lo:hi], r_recv.at[i])
     for copy in [to_twin, after, before] + to_z + to_y + to_x:
         copy.wait_send()
-    for group in range(2):
+    for group in range(3):
         for j in (0, 1):
             spread(group, j).wait_send()
         forward(group).wait_send()
@@ -549,9 +556,9 @@
             pltpu.VMEM((ncell, 32), bf16),
             pltpu.VMEM((32, nblocks * width), bf16),
             pltpu.VMEM((32, nblocks * width), f32),
-            pltpu.VMEM((4, 2, ncell // 16, nblocks * width), bf16),
+            pltpu.VMEM((6, 2, ncell // 16, nblocks * width), bf16),
             pltpu.VMEM((3, nblocks * width), f32),
-            dma((5,)), dma((2,)), dma((2,)), dma((2, 3)), dma((2, 3)), dma((3,)), dma((3,)),
+            dma((5,)), dma((2,)), dma((2,)), dma((3, 3)), dma((3, 3)), dma((3,)), dma((3,)),
             dma, dma, dma((3,)), dma((3,)), dma((3,)), dma((3,)), dma((3,)), dma((3,)), dma, dma,
         ],
         compiler_params=pltpu.CompilerParams(

time: 51.8 us -> 49.4 us (0.954)
  the two profiles are of different devices: /device:TPU:32 before, /device:TPU:8 now
where the time goes in v9:
time: 49.4 us; the launch traced here: 49.3 us
  Pallas kernels  48.4 us (98%)
  between operations  0.84 us (2%)
    pallas_call x1, Pallas kernels, on_device(): pl.pallas_call(exchange_and_far, out_shape=(jax.ShapeDtypeStruct((3, nblo...  33.4 us
    pallas_call x1, Pallas kernels, on_device(): pl.pallas_call(near_kernel, out_shape=jax.ShapeDtypeStruct((3, nblocks, w...  15 us

profile of v9, /device:TPU:8, one launch (start us, length us, event | category | flops | bytes accessed | tf_op | source)
XLA Modules:
  0.0 49.3 jit_solution(17598453115779572557)
XLA Ops:
  0.7 33.4 %shard_map.55 = (f32[3,4096]{1,0:T(4,128)}, f32[2,12,296,128]{3,2,1,0:T(8,128)}) custom-call(f32[9,32,128]{2,1,0:T(8,128)} %bitcast.10, s32[1,32]{1,0:T(1,128)} %bitcast.12, f32[3,4096]{1,0:T(4,128)} %cc_hbm.1, s32[2,128]{1,0:T(2,128)} %bitcast.11, s32[1,1]{1,0:T(1,128)} %bitcast.7.live_hbm), custom_call_target="tpu_custom_call" | custom-call | tf_op jit(solution)/shard_map/pallas_call | solution.py:534
  34.1 15.0 %shard_map.56 = f32[3,32,128]{2,1,0:T(8,128)} custom-call(f32[7104,128]{1,0:T(8,128)} %bitcast.8, f32[24,296,128]{2,1,0:T(8,128)} %bitcast.9, f32[3,4096]{1,0:T(4,128)} %get-tuple-element.8.far_hbm), custom_call_target="tpu_custom_call" | custom-call | tf_op jit(solution)/shard_map/pallas_call | solution.py:571

commit v10 on v9

--- a/solution.py
+++ b/solution.py
@@ -403,10 +403,9 @@
     row8 = lax.broadcasted_iota(jnp.int32, (8, 128), 0)
     ends = starts + even
 
-    def fill(kr, carry):
+    def rows_of(kr):
         got = jnp.zeros((8, 128), f32)
-        first = (kr * 128).astype(f32)
-        want = lane + first
+        want = lane + (kr * 128).astype(f32)
         for r in range(25):
             hot = (rank_t[:, r : r + 1] == want).astype(bf16)
             vals = jnp.where(row8 == 0, dev[r : r + 1], jnp.where(row8 == 1, local[r : r + 1], 1.0))
@@ -418,14 +417,22 @@
         rows = jnp.where(
             row8 == 0, other, jnp.where(row8 == 1, own, jnp.where(row8 == 2, got[2:3], 0.0))
         )
-        listed[...] = rows.astype(jnp.int32)
-        copy = pltpu.make_async_copy(listed, table.at[pl.ds(kr * 8, 8)], sem)
+        return rows.astype(jnp.int32)
+
+    for kr in range(2):
+        listed[8 * kr : 8 * kr + 8, :] = rows_of(jnp.int32(kr))
+    first = pltpu.make_async_copy(listed.at[0:16], table.at[0:16], sem.at[0])
+    first.start()
+
+    def fill(kr, carry):
+        listed[16:24, :] = rows_of(kr)
+        copy = pltpu.make_async_copy(listed.at[16:24], table.at[pl.ds(kr * 8, 8)], sem.at[1])
         copy.start()
         copy.wait()
         return carry
 
-    lax.fori_loop(0, (count + 127) // 128, fill, 0)
-    return count
+    lax.fori_loop(2, lax.div(count + 127, 128), fill, 0)
+    return count, first
 
 
 def near_kernel(
@@ -442,7 +449,7 @@
     for copy in (pairs_in, own_in, win_in, far_in):
         copy.start()
     pairs_in.wait()
-    count = build_list(pair_ref, space, sub, nblocks, hots, listed, table, sem)
+    count, listing = build_list(pair_ref, space, sub, nblocks, hots, listed, table, sem)
     own_in.wait()
     origin = jnp.where(
         lax.broadcasted_iota(jnp.int32, (16, 1), 0) < 3, own_ref[0:16, 0:1], 0.0
@@ -467,6 +474,7 @@
             feats[q + g, :, 0:128] = f[0:128, g * 128 : g * 128 + 128]
             feats[q + g, :, 128:256] = f[128:256, g * 128 : g * 128 + 128]
 
+    listing.wait()
     win_in.wait()
     top = lax.broadcasted_iota(jnp.int32, (16, 128), 0) < 3
 
@@ -583,9 +591,9 @@
             pltpu.VMEM((nblocks, width), f32),
             pltpu.VMEM((nblocks, 16, width), f32),
             pltpu.VMEM((25 * 32, width), f32),
-            pltpu.VMEM((8, width), jnp.int32),
+            pltpu.VMEM((24, width), jnp.int32),
             pltpu.SMEM((26 * 8, width), jnp.int32),
-            dma, dma((4,)),
+            dma((2,)), dma((4,)),
         ],
         compiler_params=pltpu.CompilerParams(vmem_limit_bytes=56 << 20),
     )(window.reshape(24 * ROWS, width), window.reshape(24, ROWS, width), far)

time: 49.4 us -> 46.6 us (0.943)
  the two profiles are of different devices: /device:TPU:8 before, /device:TPU:0 now
where the time goes in v10:
time: 46.6 us; the launch traced here: 46.5 us
  Pallas kernels  45.6 us (98%)
  between operations  0.84 us (2%)
    pallas_call x1, Pallas kernels, on_device(): pl.pallas_call(exchange_and_far, out_shape=(jax.ShapeDtypeStruct((3, nblo...  34.5 us
    pallas_call x1, Pallas kernels, on_device(): pl.pallas_call(near_kernel, out_shape=jax.ShapeDtypeStruct((3, nblocks, w...  11.1 us

profile of v10, /device:TPU:0, one launch (start us, length us, event | category | flops | bytes accessed | tf_op | source)
XLA Modules:
  0.0 46.5 jit_solution(17611641738612835504)
XLA Ops:
  0.7 34.5 %shard_map.55 = (f32[3,4096]{1,0:T(4,128)}, f32[2,12,296,128]{3,2,1,0:T(8,128)}) custom-call(f32[9,32,128]{2,1,0:T(8,128)} %bitcast.10, s32[1,32]{1,0:T(1,128)} %bitcast.12, f32[3,4096]{1,0:T(4,128)} %cc_hbm.1, s32[2,128]{1,0:T(2,128)} %bitcast.11, s32[1,1]{1,0:T(1,128)} %bitcast.7.live_hbm), custom_call_target="tpu_custom_call" | custom-call | tf_op jit(solution)/shard_map/pallas_call | solution.py:542
  35.2 11.1 %shard_map.56 = f32[3,32,128]{2,1,0:T(8,128)} custom-call(f32[7104,128]{1,0:T(8,128)} %bitcast.8, f32[24,296,128]{2,1,0:T(8,128)} %bitcast.9, f32[3,4096]{1,0:T(4,128)} %get-tuple-element.8.far_hbm), custom_call_target="tpu_custom_call" | custom-call | tf_op jit(solution)/shard_map/pallas_call | solution.py:579

commit v11 on v10

--- a/solution.py
+++ b/solution.py
@@ -239,7 +239,6 @@
         for j in (0, 1):
             spread(group, j).start()
     lax.fori_loop(4, 6, make, 0)
-    acc[...] = product(0, 0, early[0, 0], early[0, 1])
 
     for k in range(3):
         arrived(moments.at[0, k + 1], y_recv.at[k])
@@ -248,6 +247,7 @@
     for j in (0, 1):
         arrived(place(0, j + 1), z_recv.at[0, j])
     forward(0).start()
+    acc[...] = product(0, 0, early[0, 0], early[0, 1])
     acc[...] += (
         product(0, 1, early[1, 0], early[1, 1])
         + product(0, 2, early[2, 0], early[2, 1])

time: 46.6 us -> 46.7 us (level)
  the two profiles are of different devices: /device:TPU:0 before, /device:TPU:64 now
where the time goes in v11:
time: 46.7 us; the launch traced here: 46.2 us
  Pallas kernels  45.4 us (97%)
  between operations  0.84 us (2%)
    pallas_call x1, Pallas kernels, on_device(): pl.pallas_call(exchange_and_far, out_shape=(jax.ShapeDtypeStruct((3, nblo...  32.1 us
    pallas_call x1, Pallas kernels, on_device(): pl.pallas_call(near_kernel, out_shape=jax.ShapeDtypeStruct((3, nblocks, w...  13.2 us

profile of v11, /device:TPU:64, one launch (start us, length us, event | category | flops | bytes accessed | tf_op | source)
XLA Modules:
  0.0 46.2 jit_solution(9521089669014517820)
XLA Ops:
  0.7 32.1 %shard_map.55 = (f32[3,4096]{1,0:T(4,128)}, f32[2,12,296,128]{3,2,1,0:T(8,128)}) custom-call(f32[9,32,128]{2,1,0:T(8,128)} %bitcast.10, s32[1,32]{1,0:T(1,128)} %bitcast.12, f32[3,4096]{1,0:T(4,128)} %cc_hbm.1, s32[2,128]{1,0:T(2,128)} %bitcast.11, s32[1,1]{1,0:T(1,128)} %bitcast.7.live_hbm), custom_call_target="tpu_custom_call" | custom-call | tf_op jit(solution)/shard_map/pallas_call | solution.py:542
  32.8 13.2 %shard_map.56 = f32[3,32,128]{2,1,0:T(8,128)} custom-call(f32[7104,128]{1,0:T(8,128)} %bitcast.8, f32[24,296,128]{2,1,0:T(8,128)} %bitcast.9, f32[3,4096]{1,0:T(4,128)} %get-tuple-element.8.far_hbm), custom_call_target="tpu_custom_call" | custom-call | tf_op jit(solution)/shard_map/pallas_call | solution.py:579
